TPU v7x, 512 devices: a whole 4x8x8 slice. The times are simulated.
512 devices in a mesh: dp: 128 (over z, y, core), owner: 4 (over x).
Axes of the slice: x: 4, y: 8, z: 8, core: 2. Of those that a mesh axis runs over, the one named last changes fastest.
Arguments:
- block_input: bfloat16 [131072, 512], P('dp', 'owner'), may hold values from -6 to 6
- block_middle: bfloat16 [131072, 512], P('dp', 'owner'), may hold values from -6 to 6
- out_grad: bfloat16 [131072, 512], P('dp', 'owner'), may hold values from -0.03125 to 0.03125
- lengths: int32 [256], P('dp'), may hold values from 1 to 512, 98304 in all
- conv_weight: bfloat16 [512, 5, 512], P(None, None, 'owner'), may hold values from -0.125 to 0.125
- block_of_slot: int32 [128], replicated, may hold values from 0 to 39, as said below
- slot_count: int32 [128], P('dp'), may hold values from 0 to 1, as said below
- left_prev: float32 [128, 16384], P('dp'), as said below
- right_prev: float32 [128, 65536], P('dp', 'owner'), as said below
Outputs:
- update: float32 [128, 65536], P('dp', 'owner')
Inputs may be any that keep to these rules, and one draw needn't show every extreme that they name: `block_of_slot`: group g owns slots g * 1 to (g + 1) - 1; its first slot_count[g] slots are used. The used slots of all groups name every block exactly once; unused slots hold some block number. `slot_count`: the counts sum to 40. `left_prev`: each 128 x 128 block is symmetric positive definite. `right_prev`: each 128 x 128 block is symmetric positive definite.
All inputs are finite; a program needn't handle non-finite values. No bound on the sum of `lengths` on one device may be relied on, other than what follows from the above.
Results may differ from a plain program's by a relative error of at most 0.01.
Values may be sent and summed in bfloat16 or wider, within the bound.
A program may use at most 64 MiB of HBM per device.

v0:
```python
import jax
import jax.numpy as jnp
from jax import lax
from jax.sharding import PartitionSpec as P

KW = 5
FIRST_DILATION1 = 4
SECOND_DILATION2 = 8
BR = 128
ITERS = 8


decay_rate = 0.9


def shift_rows(values, offset):
    seq_length = values.shape[1]
    margin = abs(offset)
    padded = jnp.pad(values, ((0, 0), (margin, margin), (0, 0)))
    return padded[:, margin + offset : margin + offset + seq_length]


def stacked_taps(gradient, dilation):
    middle = KW // 2
    shifted_list = [shift_rows(gradient, -(tap - middle) * dilation) for tap in range(KW)]
    first_stacked = jnp.concatenate(shifted_list, axis=2)
    return first_stacked.reshape(-1, first_stacked.shape[2])


def kernel_gradient(activations, first_stacked, out_width):
    product = lax.dot_general(
        activations, first_stacked, (((0,), (0,)), ((), ())), preferred_element_type=jnp.float32
    )
    return product.reshape(activations.shape[1] * (first_stacked.shape[1] // out_width), out_width)


def gelu_slope(values):
    return (
        0.5 * (1.0 + lax.erf(values * 0.7071067811865476))
        + values * jnp.exp(-0.5 * values * values) * 0.3989422804014327
    )


def batch_product(left, right):
    return jnp.einsum("...ij,...jk->...ik", left, right, precision=lax.Precision.HIGHEST)


def inverse_fourth_root(statistic):
    order_size = statistic.shape[-1]
    identity_mat = jnp.eye(order_size, dtype=jnp.float32)
    frob_norm = jnp.sqrt(jnp.sum(statistic * statistic, axis=(-2, -1)))[..., None, None]
    current = statistic / frob_norm
    root_mat = jnp.broadcast_to(identity_mat, statistic.shape)
    for iteration in range(ITERS):
        factor = (5.0 * identity_mat - current) * 0.25
        square = batch_product(factor, factor)
        fourth = batch_product(square, square)
        current = batch_product(fourth, current)
        root_mat = batch_product(root_mat, factor)
    return root_mat * frob_norm ** (-0.25)


def local(
    block_input,
    block_middle,
    out_grad,
    lengths,
    conv_weight,
    block_of_slot,
    slot_count,
    left_prev,
    right_prev,
):
    seq_count = lengths.shape[0]
    row_count, narrow_slice = block_input.shape
    seq_len = row_count // seq_count
    positions = lax.broadcasted_iota(jnp.int32, (seq_count, seq_len), 1)
    valid_mask = (positions < lengths[:, None]).astype(jnp.float32)[:, :, None]
    full_input, full_middle = (
        lax.all_gather(block_input, "owner", axis=1, tiled=True),
        lax.all_gather(block_middle, "owner", axis=1, tiled=True),
    )
    full_width = full_input.shape[1]

    def activate(values):
        shaped = values.astype(jnp.float32).reshape(seq_count, seq_len, full_width)
        return (
            (jax.nn.gelu(shaped, approximate=False) * valid_mask)
            .astype(jnp.bfloat16)
            .reshape(row_count, full_width)
        )

    first_hidden = activate(full_input)
    second_hidden = activate(full_middle)
    second_gradient = (
        out_grad.astype(jnp.float32).reshape(seq_count, seq_len, narrow_slice) * valid_mask
    ).astype(jnp.bfloat16)
    second_stacked = stacked_taps(second_gradient, SECOND_DILATION2)
    weight_two = kernel_gradient(second_hidden, second_stacked, narrow_slice)
    flat_weight = conv_weight.reshape(full_width, KW * narrow_slice)
    partial_value = lax.dot_general(
        second_stacked, flat_weight, (((1,), (1,)), ((), ())), preferred_element_type=jnp.float32
    )
    back_two = lax.psum_scatter(
        partial_value.astype(jnp.bfloat16), "owner", scatter_dimension=1, tiled=True
    ).astype(jnp.float32)
    slope_vals = gelu_slope(
        block_middle.astype(jnp.float32).reshape(seq_count, seq_len, narrow_slice)
    )
    first_gradient = (
        second_gradient.astype(jnp.float32)
        + slope_vals * valid_mask * back_two.reshape(seq_count, seq_len, narrow_slice)
    ).astype(jnp.bfloat16)
    first_weight = kernel_gradient(
        first_hidden, stacked_taps(first_gradient, FIRST_DILATION1), narrow_slice
    )
    flat_grads = jnp.stack([first_weight, weight_two]).reshape(-1, narrow_slice)
    capacity = left_prev.shape[0]
    own_ids = lax.dynamic_slice_in_dim(block_of_slot, lax.axis_index("dp") * capacity, capacity, 0)
    totals = lax.psum(flat_grads, "dp")
    block_tiles = totals.reshape(-1, BR, narrow_slice)[own_ids]
    left_part = batch_product(block_tiles, jnp.swapaxes(block_tiles, 1, 2))
    left_sum = lax.psum(left_part.astype(jnp.bfloat16), "owner").astype(jnp.float32)
    left_stat = decay_rate * left_prev.reshape(capacity, BR, BR) + (1.0 - decay_rate) * left_sum
    right_stat = decay_rate * right_prev.reshape(capacity, narrow_slice, narrow_slice) + (
        1.0 - decay_rate
    ) * batch_product(jnp.swapaxes(block_tiles, 1, 2), block_tiles)
    left_root = inverse_fourth_root(left_stat)
    right_root = inverse_fourth_root(right_stat)
    mixed = batch_product(left_root, block_tiles) + batch_product(block_tiles, right_root)
    raw_update = batch_product(left_root, mixed) + batch_product(mixed, right_root)
    squares = lax.psum(jnp.sum(raw_update * raw_update, axis=(1, 2)), "owner")
    inverse_rms = 1.0 / jnp.sqrt(squares / (lax.axis_size("owner") * BR * narrow_slice) + 1e-06)
    live_slots = jnp.arange(capacity, dtype=jnp.int32) < slot_count[0]
    scaled = (raw_update * inverse_rms[:, None, None]).reshape(capacity, BR * narrow_slice)
    return jnp.where(live_slots[:, None], scaled, 0.0)


def solution(mesh):
    return jax.shard_map(
        local,
        mesh=mesh,
        in_specs=(
            P("dp", "owner"),
            P("dp", "owner"),
            P("dp", "owner"),
            P("dp"),
            P(None, None, "owner"),
            P(),
            P("dp"),
            P("dp", None),
            P("dp", "owner"),
        ),
        out_specs=P("dp", "owner"),
        check_vma=False,
    )
```

profile of v0, /device:TPU:26, one launch (start us, length us, event | category | flops | bytes accessed | tf_op | source)
XLA Modules:
  0.0 382.2 jit_solution(15693446058916099542)
XLA Ops:
  8.1 1.3 copy.41
  10.1 1.1 fusion.37
  11.8 1.1 copy-done.5
  13.9 1.3 copy.48
  15.4 28.9 %all-gather.3.cloned.1.call-done = bf16[1024,512]{1,0:T(8,128)(2,1)} async-done(((bf16[1024,128]{1,0:T(8,128)(2,1)}), bf16[1024,512]{1,0:T(8,128)(2,1)}) %all-gather.3.cloned.1.call-update) | async-done | bytes 1048592 | tf_op jit(solution)/shard_map/all_gather | solution.py:80
  44.4 3.1 fusion
  47.5 2.9 copy.35
  50.4 1.9 copy.40
  52.2 26.5 %all-gather.5.cloned.1.call-done = bf16[1024,512]{1,0:T(8,128)(2,1)} async-done(((bf16[1024,128]{1,0:T(8,128)(2,1)}), bf16[1024,512]{1,0:T(8,128)(2,1)}) %all-gather.5.cloned.1.call-update) | async-done | bytes 1048592 | tf_op jit(solution)/shard_map/all_gather | solution.py:81
  78.7 3.1 fusion.1
  81.8 2.9 copy.42
  84.7 1.8 copy.47
  86.6 7.0 %convolution_bitcast_fusion = f32[512,640]{1,0:T(8,128)S(1)} fusion(bf16[2,512,640]{2,1,0:T(8,128)(2,1)} %copy-done.5, f32[2,512,512]{1,2,0:T(8,128)} %copy.47, f32[2,512,512]{1,2,0:T(8,128)} %copy.42, f32[2,512]{1,0:T(2,128)S(1)} %compare_convert_fusion), kind=kOutput, calls=%fused_computation.44 | convolution fusion | flops 704118784 | bytes 6819840 | tf_op jit(solution)/shard_map/dot_general | solution.py:31
  93.7 16.6 %reduce-scatter.4.cloned.1.call-done = bf16[128,1024]{1,0:T(8,128)(2,1)} async-done(((bf16[512,1024]{1,0:T(8,128)(2,1)}), bf16[128,1024]{1,0:T(8,128)(2,1)}) %reduce-scatter.4.cloned.1.call-update) | async-done | bytes 262160
  110.3 1.1 copy.49
  113.0 7.1 %convolution_bitcast_fusion.1 = f32[512,640]{1,0:T(8,128)} fusion(bf16[2,512,640]{2,1,0:T(8,128)(2,1)S(1)} %slice_dynamic-update-slice_fusion, f32[2,512,512]{1,2,0:T(8,128)} %copy.40, f32[2,512,512]{1,2,0:T(8,128)S(1)} %copy-done.1, f32[2,512]{1,0:T(2,128)S(1)} %compare_convert_fusion), kind=kOutput, calls=%fused_computation.45 | convolution fusion | flops 704118784 | bytes 6819840 | tf_op jit(solution)/shard_map/dot_general | solution.py:31
  120.0 1.4 stack_reshape.6
  121.4 1.7 pad_maximum_fusion
  127.2 200.5 %all-reduce.6.cloned.1.call-done = f32[40,128,128]{2,1,0:T(8,128)} async-done(((f32[40,128,128]{2,1,0:T(8,128)}), f32[40,128,128]{2,1,0:T(8,128)}) %all-reduce.6.cloned.1.call-update) | async-done | bytes 2621456 | tf_op jit(solution)/shard_map/psum | solution.py:120
  327.7 1.9 multiply_reduce_fusion.1
  330.7 1.2 fusion.25
  331.9 14.1 %psum.22 = bf16[1,128,128]{2,1,0:T(8,128)(2,1)S(1)} all-reduce(bf16[1,128,128]{2,1,0:T(8,128)(2,1)S(1)} %fusion.25), channel_id=1, replica_groups=mesh['dp'=128,'owner'=4] {'owner'}, use_global_device_ids=true, to_apply=%region_2.3 | all-reduce | flops 16384 | bytes 65536 | tf_op jit(solution)/shard_map/psum | solution.py:123
  360.5 1.0 convolution_add_fusion.1
  362.6 11.8 %psum.23 = f32[1]{0:T(128)} all-reduce(f32[1]{0:T(128)} %bitcast.21), channel_id=1, replica_groups=mesh['dp'=128,'owner'=4] {'owner'}, use_global_device_ids=true, to_apply=%region_6.7 | all-reduce | flops 1 | bytes 8 | tf_op jit(solution)/shard_map/psum | solution.py:132
  (101 shorter events, 22.3 us)
Async XLA Ops:
  6.5 4.9 %copy-start = (bf16[1024,128]{1,0:T(8,128)(2,1)S(1)}, bf16[1024,128]{1,0:T(8,128)(2,1)}, u32[]{:S(2)}) copy-start(bf16[1024,128]{1,0:T(8,128)(2,1)} %param.11) | copy-start | bytes 786436
  6.5 37.8 %all-gather.3.cloned.1.call-start = ((), (), s32[]{:S(2)}) async-start(), calls=%async_computation.1 | async-start | bytes 1310720 | tf_op jit(solution)/shard_map/all_gather | solution.py:80
  7.3 71.5 %all-gather.5.cloned.1.call-start = ((), (), s32[]{:S(2)}) async-start(), calls=%async_computation.2 | async-start | bytes 1310720 | tf_op jit(solution)/shard_map/all_gather | solution.py:81
  8.0 102.2 %reduce-scatter.4.cloned.1.call-start = ((), (), s32[]{:S(2)}) async-start(), calls=%async_computation.4 | async-start | bytes 1310720
  11.8 1.1 copy-start.5
  13.9 1.4 copy-start.3
  15.3 312.4 %all-reduce.6.cloned.1.call-start = ((), (), s32[]{:S(2)}) async-start(), calls=%async_computation.3 | async-start | bytes 5242880 | tf_op jit(solution)/shard_map/psum | solution.py:120
  93.5 17.8 %copy-start.2 = (bf16[1024,128]{1,0:T(8,128)(2,1)S(1)}, bf16[1024,128]{1,0:T(8,128)(2,1)}, u32[]{:S(2)}) copy-start(bf16[1024,128]{1,0:T(8,128)(2,1)} %param.10) | copy-start | bytes 786436
  111.4 1.6 copy-start.1
  123.1 0.8 copy-start.4
  123.1 0.9 copy-start.6
Sparse Core Ops, SparseCore 0:
  9.4 34.8 all-gather.2
  46.5 32.2 all-gather.4
  81.6 28.6 reduce-scatter.3
  123.2 204.4 all-reduce.5
where the time goes:
time: 383 us; the launch traced here: 382 us
  waiting for transfers between devices  274 us (72%)
  matrix products  33.1 us (9%)
  blocking collectives  25.9 us (7%)
  local copies, waits for them, and re-layouts  18.7 us (5%)
  between operations  18.6 us (5%)
  other arithmetic  11.8 us (3%)
    psum x1, waiting for transfers between devices, local(): totals = lax.psum(flat_grads, 'dp')  200 us
    all_gather x1, waiting for transfers between devices, local(): lax.all_gather(block_input, 'owner', axis=1, tiled=True)  28.9 us
    all_gather x1, waiting for transfers between devices, local(): lax.all_gather(block_middle, 'owner', axis=1, tiled=True)  26.5 us
    dot_general x64, matrix products, batch_product(): jnp.einsum('...ij,...jk->...ik', left, right, precision=lax.Precision.HIG...  18.1 us
    unnamed x5, waiting for transfers between devices  18 us
    psum x1, blocking collectives, local(): lax.psum(left_part.astype(jnp.bfloat16), 'owner').astype(jnp.float32)  14.1 us
    dot_general x2, matrix products, kernel_gradient(): lax.dot_general(activations, first_stacked, (((0,), (0,)), ((), ())), pre...  14 us
    psum x1, blocking collectives, local(): squares = lax.psum(jnp.sum(raw_update * raw_update, axis=(1, 2)), 'owner')  11.8 us
  transfers between devices with their start and end apart: 4, of which 4 were waited for; matrix products, arithmetic and copies ran while one was open for 8% of the time, Pallas kernels for 0%

commit v1 on v0

v1 whole, which is shorter than its diff:
```python
import jax
import jax.numpy as jnp
from jax import lax
from jax.experimental import pallas as pl
from jax.experimental.pallas import tpu as pltpu
from jax.sharding import PartitionSpec as P

MESH = pl.DeviceIdType.MESH
F32, BF16 = jnp.float32, jnp.bfloat16
KW = 5
BR = 128
LEN = 512
PAD = 16
NS = 2
NX, NY, NZ = 4, 8, 8
ITERS = 8
DECAY = 0.9
HIGH = lax.Precision.HIGHEST


def mm(a, b):
    return jnp.dot(a, b, precision=HIGH, preferred_element_type=F32)


def inverse_fourth_roots(stats):
    rows = lax.broadcasted_iota(jnp.int32, (BR, BR), 0)
    cols = lax.broadcasted_iota(jnp.int32, (BR, BR), 1)
    eye = (rows == cols).astype(F32)
    norms = [jnp.sqrt(jnp.sum(s * s, axis=(0, 1), keepdims=True)) for s in stats]
    cur = [s / n for s, n in zip(stats, norms)]
    root = None
    for it in range(ITERS):
        fac = [(5.0 * eye - m) * 0.25 for m in cur]
        root = fac if it == 0 else [mm(r, f) for r, f in zip(root, fac)]
        if it < ITERS - 1:
            square = [mm(f, f) for f in fac]
            fourth = [mm(s, s) for s in square]
            cur = [mm(f, m) for f, m in zip(fourth, cur)]
    scale = [1.0 / jnp.sqrt(jnp.sqrt(n)) for n in norms]
    return [r * s for r, s in zip(root, scale)]


def peer_at(major, minor, core):
    z = major + core * (minor - major)
    y = minor + core * (major - minor)
    return (z * NY + y) * 2 + core


def kernel(
    x1_ref, x2_ref, g_ref, len_ref, w_ref, bos_ref, cnt_ref, lprev_ref, rprev_ref, out_ref,
    gbuf, hbuf, h2t, slope, wbuf, gst, g1, back, kbuf,
    c0, p1, r1, u1, p2, r2, p3, r3, rows_ref, d3, e3, d4, f4, tile_ref, lp, lr, sq, sr,
    gs_sem, gr_sem, hs_sem, hr_sem, ws_sem, wr_sem, c0_sem, s1_sem, r1_sem, s2_sem, r2_sem,
    s3_sem, r3_sem, ds_sem, dr_sem, fs_sem, fr_sem, ls_sem, lr_sem, qs_sem, qr_sem,
):
    dp, p = lax.axis_index("dp"), lax.axis_index("owner")
    c = dp % 2
    y = (dp // 2) % NY
    z = dp // (2 * NY)
    a = z + c * (y - z)
    b = y + c * (z - y)
    right, left = (p + 1) % NX, (p + 3) % NX

    def rcopy(src, dst, ss, rs, dev):
        return pltpu.make_async_remote_copy(
            src_ref=src, dst_ref=dst, send_sem=ss, recv_sem=rs, device_id=dev, device_id_type=MESH
        )

    barrier = pltpu.get_barrier_semaphore()

    def greet(dev):
        pl.semaphore_signal(barrier, inc=1, device_id=dev, device_id_type=MESH)

    @pl.loop(1, NX)
    def _(i):
        greet((dp, (p + i) % NX))

    @pl.loop(1, 2 * NZ)
    def _(i):
        k = (z * 2 + c + i) % (2 * NZ)
        greet((((k // 2) * NY + y) * 2 + k % 2, p))

    @pl.loop(0, 2 * (NY - 1))
    def _(i):
        greet(((z * NY + (y + 1 + i // 2) % NY) * 2 + i % 2, p))

    zpad = jnp.zeros((PAD, BR), BF16)
    for slot in range(NX):
        for s in range(NS):
            gbuf[slot, s, 0:PAD, :] = zpad
            gbuf[slot, s, PAD + LEN : PAD + LEN + PAD, :] = zpad
    for s in range(NS):
        g1[s, 0:PAD, :] = zpad
        g1[s, PAD + LEN : PAD + LEN + PAD, :] = zpad
    tok = lax.broadcasted_iota(jnp.int32, (LEN, BR), 0)
    for s in range(NS):
        v = g_ref[s * LEN : (s + 1) * LEN, :].astype(F32)
        gbuf[0, s, PAD : PAD + LEN, :] = jnp.where(tok < len_ref[s], v, 0.0).astype(BF16)

    pl.semaphore_wait(barrier, 3 + 15 + 14)

    def gpiece(slot, s):
        return gbuf.at[slot, s, pl.ds(PAD, LEN), :]

    def hpiece(slot, s):
        return hbuf.at[slot, s]

    plan = [
        (0, 3, 1, right), (0, 3, 0, right), (0, 1, 0, left), (0, 1, 1, left),
        (1, 2, 0, left), (3, 2, 1, right),
    ]

    def xcopy(piece, ss, rs, i):
        src, dst, s, dev = plan[i]
        return rcopy(piece(src, s), piece(dst, s), ss.at[i], rs.at[i], (dp, dev))

    def xland(piece, ss, rs, i):
        src, dst, s, dev = plan[i]
        rcopy(piece(dst, s), piece(dst, s), ss.at[i], rs.at[i], (dp, dev)).wait_recv()

    for i in (0, 2, 1, 3):
        xcopy(gpiece, gs_sem, gr_sem, i).start()

    def wcopy(i):
        q = (p + i) % NX
        src = w_ref.at[:, pl.ds(pl.multiple_of(q * BR, BR), BR), :]
        return rcopy(src, wbuf.at[NX - i], ws_sem.at[NX - i], wr_sem.at[NX - i], (dp, q))

    for i in range(1, NX):
        wcopy(i).start()
    wbuf[0] = w_ref[:, pl.ds(pl.multiple_of(p * BR, BR), BR), :]

    @pl.loop(0, NS * LEN // BR)
    def _(i):
        s = i // (LEN // BR)
        t0 = pl.multiple_of((i % (LEN // BR)) * BR, BR)
        r0 = pl.multiple_of(i * BR, BR)
        valid = (lax.broadcasted_iota(jnp.int32, (BR, BR), 0) + t0 < len_ref[s]).astype(F32)
        x = x1_ref[pl.ds(r0, BR), :].astype(F32)
        h = x * (0.5 * (1.0 + lax.erf(x * 0.7071067811865476))) * valid
        hbuf[0, s, :, pl.ds(t0, BR)] = h.T.astype(BF16)
        x = x2_ref[pl.ds(r0, BR), :].astype(F32)
        phi = 0.5 * (1.0 + lax.erf(x * 0.7071067811865476))
        h2t[s, :, pl.ds(t0, BR)] = (x * phi * valid).T.astype(BF16)
        slope[pl.ds(r0, BR), :] = (phi + x * jnp.exp(-0.5 * x * x) * 0.3989422804014327) * valid

    xland(gpiece, gs_sem, gr_sem, 0)
    xcopy(gpiece, gs_sem, gr_sem, 5).start()
    xland(gpiece, gs_sem, gr_sem, 2)
    xcopy(gpiece, gs_sem, gr_sem, 4).start()
    for i in (0, 2, 1, 3):
        xcopy(hpiece, hs_sem, hr_sem, i).start()

    def stack(src, dilation):
        for s in range(NS):
            for k in range(KW):
                r0 = PAD - (k - KW // 2) * dilation
                gst[s, :, k * BR : (k + 1) * BR] = src[s, r0 : r0 + LEN, :]

    def put_rows(kk, slot, prod):
        for k in range(KW):
            kbuf[kk, slot, pl.ds(k, BR, stride=KW), :] = prod[:, k * BR : (k + 1) * BR]

    def second_piece(slot):
        stack(gbuf.at[slot], 8)
        prod = jnp.dot(h2t[0], gst[0], preferred_element_type=F32)
        prod += jnp.dot(h2t[1], gst[1], preferred_element_type=F32)
        put_rows(1, slot, prod)
        wcat = jnp.concatenate([wbuf[slot, k] for k in range(KW)], axis=1)
        for s in range(NS):
            part = lax.dot_general(gst[s], wcat, (((1,), (1,)), ((), ())), preferred_element_type=F32)
            if slot == 0:
                back[s] = part
            else:
                back[s] += part

    def wland(i):
        wcopy(NX - i).wait_recv()

    second_piece(0)
    xland(gpiece, gs_sem, gr_sem, 1)
    wland(3)
    second_piece(3)
    xland(gpiece, gs_sem, gr_sem, 3)
    wland(1)
    second_piece(1)
    xland(gpiece, gs_sem, gr_sem, 4)
    xland(gpiece, gs_sem, gr_sem, 5)
    wland(2)
    second_piece(2)

    sib = dp + 1 - 2 * c
    NT = NX * KW

    def core_copy(kk):
        other = pl.ds(pl.multiple_of((1 - c) * 64, 64), 64)
        return rcopy(
            ktile(kk).at[:, other, :], c0.at[kk], c0_sem.at[2 * kk], c0_sem.at[2 * kk + 1], (sib, p)
        )

    def ktile(kk):
        return kbuf.at[kk].reshape(NT, BR, BR)

    def major_copy(kk, t, land):
        return rcopy(
            r1.at[kk, t] if land else p1.at[kk, t], r1.at[kk, t if land else a],
            s1_sem.at[kk, t], r1_sem.at[kk, t if land else a], (peer_at(t, b, c), p),
        )

    def minor_copy(kk, t, land):
        return rcopy(
            r2.at[kk, t] if land else p2.at[kk, t], r2.at[kk, t if land else b],
            s2_sem.at[kk, t], r2_sem.at[kk, t if land else b], (peer_at(a, t, c), p),
        )

    def to_major(kk):
        core_copy(kk).wait_recv()
        mine = pl.multiple_of(c * 64, 64)

        @pl.loop(0, 8)
        def _(t):
            t8 = pl.multiple_of(t * 8, 8)
            own = ktile(kk)[:, pl.ds(mine + t8, 8), :]
            p1[kk, t] = (own + c0[kk, :, pl.ds(t8, 8), :]).reshape(NT * 8, BR).astype(BF16)

        @pl.loop(1, 8)
        def _(i):
            major_copy(kk, (a + i) % 8, False).start()

    def to_minor(kk):
        u1[kk] = p1[kk, a].astype(F32)

        @pl.loop(1, 8)
        def _(i):
            t = (a + i) % 8
            major_copy(kk, t, True).wait_recv()
            u1[kk] += r1[kk, t].astype(F32)

        for t in range(8):
            p2[kk, t, 0:NT, :] = u1[kk, pl.ds(t, NT, stride=8), :]

        @pl.loop(1, 8)
        def _(i):
            minor_copy(kk, (b + i) % 8, False).start()

    def minor_sum(kk):
        acc = p2[kk, b, 0:NT, :]
        for i in range(1, 8):
            t = (b + i) % 8
            minor_copy(kk, t, True).wait_recv()
            acc = acc + r2[kk, t, 0:NT, :]
        return acc

    core_copy(1).start()

    for s in range(NS):
        g1[s, PAD : PAD + LEN, :] = (
            gbuf[0, s, PAD : PAD + LEN, :].astype(F32) + slope[s * LEN : (s + 1) * LEN, :] * back[s]
        ).astype(BF16)
    to_major(1)
    stack(g1, 4)

    def first_piece(slot):
        prod = jnp.dot(hbuf[slot, 0], gst[0], preferred_element_type=F32)
        prod += jnp.dot(hbuf[slot, 1], gst[1], preferred_element_type=F32)
        put_rows(0, slot, prod)

    first_piece(0)
    xland(hpiece, hs_sem, hr_sem, 0)
    xcopy(hpiece, hs_sem, hr_sem, 5).start()
    xland(hpiece, hs_sem, hr_sem, 2)
    xcopy(hpiece, hs_sem, hr_sem, 4).start()
    xland(hpiece, hs_sem, hr_sem, 1)
    first_piece(3)
    xland(hpiece, hs_sem, hr_sem, 3)
    first_piece(1)
    to_minor(1)
    xland(hpiece, hs_sem, hr_sem, 4)
    xland(hpiece, hs_sem, hr_sem, 5)
    first_piece(2)
    core_copy(0).start()

    acc = minor_sum(1)
    for slot in range(NX):
        p3[slot, 0:KW, :] = acc[slot * KW : (slot + 1) * KW, :]

    def piece_copy(i, land):
        q = (p + i) % NX
        return rcopy(
            r3.at[q] if land else p3.at[i], r3.at[q if land else p],
            s3_sem.at[i], r3_sem.at[q if land else p], (dp, q),
        )

    for i in range(1, NX):
        piece_copy(i, False).start()
    to_major(0)
    for i in range(1, NX):
        piece_copy(i, True).wait_recv()
        q = (p + i) % NX
        rows_ref[pl.ds(pl.multiple_of(32 + q * 8, 8), 8), :] = r3[q]
    rows_ref[pl.ds(pl.multiple_of(32 + p * 8, 8), 8), :] = p3[0]
    to_minor(0)
    acc = minor_sum(0)
    for slot in range(NX):
        q = (p + slot) % NX
        rows_ref[pl.ds(pl.multiple_of(q * 8, 8), KW), :] = acc[slot * KW : (slot + 1) * KW, :]

    @pl.loop(0, 8)
    def _(t):
        for m in range(8):
            for core in range(2):
                zz = t + c * (m - t)
                yy = m + c * (t - m)
                u = bos_ref[(zz * NY + yy) * 2 + core]
                second = (u >= 20).astype(jnp.int32)
                r = u - 20 * second
                row = second * 32 + (r // 5) * 8 + r % 5
                d3[t, pl.ds(m * 2 + core, 1), :] = rows_ref[pl.ds(row, 1), :]

    def slot_copy(t, land):
        return rcopy(
            e3.at[t] if land else d3.at[t], e3.at[t if land else a],
            ds_sem.at[t], dr_sem.at[t if land else a], (peer_at(t, b, c), p),
        )

    @pl.loop(1, 8)
    def _(i):
        slot_copy((a + i) % 8, False).start()

    e3[a] = d3[a]

    @pl.loop(1, 8)
    def _(i):
        slot_copy((a + i) % 8, True).wait_recv()

    for i in range(16):
        d4[i] = e3[:, i, :]

    def group_copy(i):
        m, core = i // 2, i % 2
        zz = a + c * (m - a)
        yy = m + c * (a - m)
        me = c * 8 + b
        return rcopy(
            d4.at[i], f4.at[me], fs_sem.at[i], fr_sem.at[me], ((zz * NY + yy) * 2 + core, p)
        )

    def group_land(i):
        rcopy(f4.at[i], f4.at[i], fs_sem.at[i], fr_sem.at[i], (sib, p)).wait_recv()

    @pl.loop(1, 16)
    def _(i):
        group_copy((b * 2 + c + i) % 16).start()

    f4[c * 8 + b] = d4[b * 2 + c]

    @pl.loop(1, 16)
    def _(i):
        group_land((c * 8 + b + i) % 16)

    for core in range(2):
        for t in range(8):
            tile_ref[core * 64 + t * 8 : core * 64 + t * 8 + 8, :] = f4[core * 8 : core * 8 + 8, t, :]

    tile = tile_ref[...]
    tile_t = tile.T
    lp[...] = mm(tile, tile_t).astype(BF16)

    def left_copy(i, land):
        q = (p + i) % NX
        return rcopy(
            lr.at[q] if land else lp, lr.at[q if land else p],
            ls_sem.at[i], lr_sem.at[q if land else p], (dp, q),
        )

    for i in range(1, NX):
        left_copy(i, False).start()
    right_stat = DECAY * rprev_ref[...] + (1.0 - DECAY) * mm(tile_t, tile)
    left_sum = lp[...].astype(F32)
    for i in range(1, NX):
        left_copy(i, True).wait_recv()
        left_sum = left_sum + lr[(p + i) % NX].astype(F32)
    left_stat = DECAY * lprev_ref[...] + (1.0 - DECAY) * left_sum
    left_root, right_root = inverse_fourth_roots([left_stat, right_stat])
    mixed = mm(left_root, tile) + mm(tile, right_root)
    raw = mm(left_root, mixed) + mm(mixed, right_root)

    sq[...] = jnp.broadcast_to(jnp.sum(raw * raw, axis=(0, 1), keepdims=True), (8, BR))

    def square_copy(i, land):
        q = (p + i) % NX
        return rcopy(
            sr.at[q] if land else sq, sr.at[q if land else p],
            qs_sem.at[i], qr_sem.at[q if land else p], (dp, q),
        )

    for i in range(1, NX):
        square_copy(i, False).start()
    total = sq[...]
    for i in range(1, NX):
        square_copy(i, True).wait_recv()
        total = total + sr[(p + i) % NX]
    inv = 1.0 / jnp.sqrt(total[0:1, 0:1] / (NX * BR * BR) + 1e-6)
    out_ref[...] = jnp.where(cnt_ref[0] > 0, raw * inv, 0.0)

    for i in range(6):
        xcopy(gpiece, gs_sem, gr_sem, i).wait_send()
        xcopy(hpiece, hs_sem, hr_sem, i).wait_send()
    for i in range(1, NX):
        wcopy(i).wait_send()
        piece_copy(i, False).wait_send()
        left_copy(i, False).wait_send()
        square_copy(i, False).wait_send()
    for kk in range(2):
        core_copy(kk).wait_send()

    @pl.loop(1, 8)
    def _(i):
        ta, tb = (a + i) % 8, (b + i) % 8
        for kk in range(2):
            major_copy(kk, ta, False).wait_send()
            minor_copy(kk, tb, False).wait_send()
        slot_copy(ta, False).wait_send()

    @pl.loop(1, 16)
    def _(i):
        group_copy((b * 2 + c + i) % 16).wait_send()


def local(
    block_input, block_middle, out_grad, lengths, conv_weight, block_of_slot, slot_count, left_prev, right_prev
):
    vmem = pl.BlockSpec(memory_space=pltpu.VMEM)
    smem = pl.BlockSpec(memory_space=pltpu.SMEM)
    dma = pltpu.SemaphoreType.DMA
    NT = NX * KW
    out = pl.pallas_call(
        kernel,
        out_shape=jax.ShapeDtypeStruct((BR, BR), F32),
        in_specs=[vmem, vmem, vmem, smem, vmem, smem, smem, vmem, vmem],
        out_specs=vmem,
        scratch_shapes=[
            pltpu.VMEM((NX, NS, LEN + 2 * PAD, BR), BF16),
            pltpu.VMEM((NX, NS, BR, LEN), BF16),
            pltpu.VMEM((NS, BR, LEN), BF16),
            pltpu.VMEM((NS * LEN, BR), F32),
            pltpu.VMEM((NX, KW, BR, BR), BF16),
            pltpu.VMEM((NS, LEN, KW * BR), BF16),
            pltpu.VMEM((NS, LEN + 2 * PAD, BR), BF16),
            pltpu.VMEM((NS, LEN, BR), F32),
            pltpu.VMEM((2, NX, KW * BR, BR), F32),
            pltpu.VMEM((2, NT, 64, BR), F32),
            pltpu.VMEM((2, 8, NT * 8, BR), BF16),
            pltpu.VMEM((2, 8, NT * 8, BR), BF16),
            pltpu.VMEM((2, NT * 8, BR), F32),
            pltpu.VMEM((2, 8, 24, BR), F32),
            pltpu.VMEM((2, 8, 24, BR), F32),
            pltpu.VMEM((NX, 8, BR), F32),
            pltpu.VMEM((NX, 8, BR), F32),
            pltpu.VMEM((64, BR), F32),
            pltpu.VMEM((8, 16, BR), F32),
            pltpu.VMEM((8, 16, BR), F32),
            pltpu.VMEM((16, 8, BR), F32),
            pltpu.VMEM((16, 8, BR), F32),
            pltpu.VMEM((BR, BR), F32),
            pltpu.VMEM((BR, BR), BF16),
            pltpu.VMEM((NX, BR, BR), BF16),
            pltpu.VMEM((8, BR), F32),
            pltpu.VMEM((NX, 8, BR), F32),
            dma((6,)), dma((6,)), dma((6,)), dma((6,)), dma((NX,)), dma((NX,)), dma((4,)),
            dma((2, 8)), dma((2, 8)), dma((2, 8)), dma((2, 8)), dma((NX,)), dma((NX,)),
            dma((8,)), dma((8,)), dma((16,)), dma((16,)), dma((NX,)), dma((NX,)), dma((NX,)), dma((NX,)),
        ],
        compiler_params=pltpu.CompilerParams(
            collective_id=0, has_side_effects=True, vmem_limit_bytes=40 * 1024 * 1024
        ),
    )(
        block_input, block_middle, out_grad, lengths, conv_weight.transpose(1, 0, 2), block_of_slot,
        slot_count, left_prev.reshape(BR, BR), right_prev.reshape(BR, BR),
    )
    return out.reshape(1, BR * BR)


def solution(mesh):
    return jax.shard_map(
        local,
        mesh=mesh,
        in_specs=(
            P("dp", "owner"), P("dp", "owner"), P("dp", "owner"), P("dp"), P(None, None, "owner"), P(),
            P("dp"), P("dp", None), P("dp", "owner"),
        ),
        out_specs=P("dp", "owner"),
        check_vma=False,
    )
```

time: 383 us -> 96.9 us (0.25)
  the two profiles are of different devices: /device:TPU:26 before, /device:TPU:1 now
where the time goes in v1:
time: 96.9 us; the launch traced here: 96.6 us
  Pallas kernels  89 us (92%)
  local copies, waits for them, and re-layouts  6.9 us (7%)
    pallas_call x1, Pallas kernels, local(): pl.pallas_call(kernel, out_shape=jax.ShapeDtypeStruct((BR, BR), F32), in_...  89 us
    unnamed x17, local copies, waits for them, and re-layouts  6.9 us

profile of v1, /device:TPU:1, one launch (start us, length us, event | category | flops | bytes accessed | tf_op | source)
XLA Modules:
  0.0 96.6 jit_solution(11900301947419594417)
XLA Ops:
  0.7 0.0 copy-start.6
  0.7 0.0 copy-start.7
  0.7 0.6 copy-done.6
  1.3 0.0 copy-done.7
  1.3 0.0 copy-start
  1.3 1.1 %copy-done = bf16[512,5,128]{2,0,1:T(8,128)(2,1)S(1)} copy-done((bf16[512,5,128]{2,0,1:T(8,128)(2,1)S(1)}, bf16[512,5,128]{2,0,1:T(8,128)(2,1)}, u32[]{:S(2)}) %copy-start) | copy-done | bytes 655384
  2.4 0.0 copy-start.1
  2.4 0.9 copy-done.1
  3.4 0.0 copy-start.2
  3.4 0.9 copy-done.2
  4.3 0.0 copy-start.3
  4.3 0.9 copy-done.3
  5.3 0.0 copy-start.4
  5.3 0.8 copy-done.4
  6.1 0.0 copy-start.5
  6.1 0.8 copy-done.5
  6.9 89.0 %shard_map.91 = f32[128,128]{1,0:T(8,128)S(1)} custom-call(bf16[1024,128]{1,0:T(8,128)(2,1)S(1)} %copy-done.1, bf16[1024,128]{1,0:T(8,128)(2,1)S(1)} %copy-done.2, bf16[1024,128]{1,0:T(8,128)(2,1)S(1)} %copy-done.3, s32[2]{0:T(128)S(1)} %copy-done.6, bf16[5,512,128]{2,1,0:T(8,128)(2,1)S(1)} %bitcast.4, s32[128]{0:T(128)S(1)} %copy-done.7, ...), custom_call_target="tpu_custom_call" | custom-call | tf_op jit(solution)/shard_map/pallas_call | solution.py:437
  95.9 0.6 copy.12
Async XLA Ops:
  0.7 0.7 copy-start.6
  0.7 0.7 copy-start.7
  1.3 1.1 %copy-start = (bf16[512,5,128]{2,0,1:T(8,128)(2,1)S(1)}, bf16[512,5,128]{2,0,1:T(8,128)(2,1)}, u32[]{:S(2)}) copy-start(bf16[512,5,128]{2,0,1:T(8,128)(2,1)} %param.13) | copy-start | bytes 1966084
  2.4 0.9 copy-start.1
  3.4 0.9 copy-start.2
  4.3 0.9 copy-start.3
  5.3 0.8 copy-start.4
  6.1 0.8 copy-start.5

commit v2 on v1

v2 whole, which is shorter than its diff:
```python
import jax
import jax.numpy as jnp
from jax import lax
from jax.experimental import pallas as pl
from jax.experimental.pallas import tpu as pltpu
from jax.sharding import PartitionSpec as P

MESH = pl.DeviceIdType.MESH
F32, BF16 = jnp.float32, jnp.bfloat16
KW = 5
BR = 128
LEN = 512
PAD = 16
NS = 2
NX, NY, NZ = 4, 8, 8
ITERS = 8
DECAY = 0.9


def split(a):
    high = a.astype(BF16)
    return high, (a - high.astype(F32)).astype(BF16)


def mm(a, b):
    (ah, al), (bh, bl) = a, b
    left = jnp.concatenate([ah, al], axis=1)
    right = jnp.concatenate(
        [jnp.concatenate([bh, bl], axis=1), jnp.concatenate([bh, jnp.zeros_like(bl)], axis=1)], axis=0
    )
    both = jnp.dot(left, right, preferred_element_type=F32)
    return both[:, :BR] + both[:, BR:]


def inverse_fourth_roots(stats):
    rows = lax.broadcasted_iota(jnp.int32, (BR, BR), 0)
    cols = lax.broadcasted_iota(jnp.int32, (BR, BR), 1)
    eye = (rows == cols).astype(F32)
    norms = [jnp.sqrt(jnp.sum(s * s, axis=(0, 1), keepdims=True)) for s in stats]
    cur = [s / n for s, n in zip(stats, norms)]
    root = None
    for it in range(ITERS):
        fac = [1.25 * eye - 0.25 * m for m in cur]
        parts = [split(f) for f in fac]
        if it < ITERS - 1:
            square = [split(mm(f, f)) for f in parts]
            fourth = [split(mm(s, s)) for s in square]
            cur = [mm(f, split(m)) for f, m in zip(fourth, cur)]
        root = fac if it == 0 else [mm(split(r), f) for r, f in zip(root, parts)]
    scale = [1.0 / jnp.sqrt(jnp.sqrt(n)) for n in norms]
    return [r * s for r, s in zip(root, scale)]


def peer_at(major, minor, core):
    z = major + core * (minor - major)
    y = minor + core * (major - minor)
    return (z * NY + y) * 2 + core


PLACES = (0, 3, 1, 2)
UNITS = ((1, 0, 4), (0, 0, 3), (0, 3, 1))


def padded_rows(places):
    return -(-places * KW * 8 // 16) * 16


def kernel(
    x1_hbm, x2_hbm, g_hbm, len_ref, w_ref, bos_ref, cnt_ref, lprev_hbm, rprev_hbm, out_ref,
    x1_ref, x2_ref, g_ref, lprev_ref, rprev,
    gbuf, hbuf, h2t, slope, wbuf, gst, g1, kbuf,
    c0, c1, c2, pa0, pa1, pa2, ra0, ra1, ra2, pb0, pb1, pb2, rb0, rb1, rb2, p3, r3, rows_ref, d4, f4, tiles,
    gs_sem, gr_sem, hs_sem, hr_sem, ws_sem, wr_sem, as_sem, ar_sem, c0_sem, s1_sem, r1_sem, s2_sem, r2_sem,
    s3_sem, r3_sem, fs_sem, fr_sem, vs_sem, vr_sem, ts_sem, tr_sem, in_sem,
):
    dp, p = lax.axis_index("dp"), lax.axis_index("owner")
    c = dp % 2
    y = (dp // 2) % NY
    z = dp // (2 * NY)
    a = z + c * (y - z)
    b = y + c * (z - y)
    right, left = (p + 1) % NX, (p + 3) % NX
    core_in, pa, ra = (c0, c1, c2), (pa0, pa1, pa2), (ra0, ra1, ra2)
    pb, rb = (pb0, pb1, pb2), (rb0, rb1, rb2)

    def rcopy(src, dst, ss, rs, dev):
        return pltpu.make_async_remote_copy(
            src_ref=src, dst_ref=dst, send_sem=ss, recv_sem=rs, device_id=dev, device_id_type=MESH
        )

    def fetch(i, src, dst):
        return pltpu.make_async_copy(src, dst, in_sem.at[i])

    own = pl.ds(pl.multiple_of(p * BR, BR), BR)
    fetches = [
        fetch(0, g_hbm, g_ref), fetch(1, x1_hbm, x1_ref), fetch(2, x2_hbm, x2_ref),
        fetch(3, w_ref.at[:, own, :], wbuf.at[0]), fetch(4, lprev_hbm, lprev_ref), fetch(5, rprev_hbm, rprev.at[0]),
    ]
    for f in fetches:
        f.start()

    sent, loops = [], []

    def send(copy):
        copy.start()
        sent.append(copy)

    def drain():
        for copy in sent:
            copy.wait_send()
        for count, copy in loops:

            @pl.loop(1, count)
            def _(i):
                copy(i).wait_send()

    barrier = pltpu.get_barrier_semaphore()

    def greet(dev):
        pl.semaphore_signal(barrier, inc=1, device_id=dev, device_id_type=MESH)

    @pl.loop(1, NX)
    def _(i):
        greet((dp, (p + i) % NX))

    @pl.loop(1, 2 * NZ)
    def _(i):
        k = (z * 2 + c + i) % (2 * NZ)
        greet((((k // 2) * NY + y) * 2 + k % 2, p))

    @pl.loop(0, 2 * (NY - 1))
    def _(i):
        greet(((z * NY + (y + 1 + i // 2) % NY) * 2 + i % 2, p))

    zpad = jnp.zeros((PAD, BR), BF16)
    for slot in range(NX):
        for s in range(NS):
            gbuf[slot, s, 0:PAD, :] = zpad
            gbuf[slot, s, PAD + LEN : PAD + LEN + PAD, :] = zpad
    for s in range(NS):
        g1[s, 0:PAD, :] = zpad
        g1[s, PAD + LEN : PAD + LEN + PAD, :] = zpad
    tok = lax.broadcasted_iota(jnp.int32, (LEN, BR), 0)
    fetches[0].wait()
    for s in range(NS):
        v = g_ref[s * LEN : (s + 1) * LEN, :].astype(F32)
        gbuf[0, s, PAD : PAD + LEN, :] = jnp.where(tok < len_ref[s], v, 0.0).astype(BF16)

    pl.semaphore_wait(barrier, 3 + 15 + 14)

    def gpiece(slot, s):
        return gbuf.at[slot, s, pl.ds(PAD, LEN), :]

    def hpiece(slot, s):
        return hbuf.at[slot, s]

    plan = [
        (0, 3, 1, right), (0, 3, 0, right), (0, 1, 0, left), (0, 1, 1, left),
        (1, 2, 0, left), (3, 2, 1, right),
    ]

    def xcopy(piece, ss, rs, i):
        src, dst, s, dev = plan[i]
        return rcopy(piece(src, s), piece(dst, s), ss.at[i], rs.at[i], (dp, dev))

    def xland(piece, ss, rs, i):
        src, dst, s, dev = plan[i]
        rcopy(piece(dst, s), piece(dst, s), ss.at[i], rs.at[i], (dp, dev)).wait_recv()

    def wcopy(i):
        q = (p + i) % NX
        src = w_ref.at[:, pl.ds(pl.multiple_of(q * BR + a * 16, 16), 16), :]
        dst = wbuf.at[NX - i, :, pl.ds(pl.multiple_of(a * 16, 16), 16), :]
        return rcopy(src, dst, ws_sem.at[NX - i], wr_sem.at[NX - i], (dp, q))

    def wpart(t):
        return wbuf.at[pl.ds(1, NX - 1), :, pl.ds(pl.multiple_of(t * 16, 16), 16), :]

    def wspread(i):
        t = (a + i) % 8
        return rcopy(wpart(a), wpart(a), as_sem.at[t], ar_sem.at[a], (peer_at(t, b, c), p))

    def wspread_land(i):
        t = (a + i) % 8
        rcopy(wpart(t), wpart(t), as_sem.at[t], ar_sem.at[t], (peer_at(t, b, c), p)).wait_recv()

    for i in range(1, NX):
        send(wcopy(i))
    for i in (0, 2, 1, 3):
        send(xcopy(gpiece, gs_sem, gr_sem, i))

    fetches[1].wait()

    @pl.loop(0, NS * LEN // BR)
    def _(i):
        s = i // (LEN // BR)
        t0 = pl.multiple_of((i % (LEN // BR)) * BR, BR)
        r0 = pl.multiple_of(i * BR, BR)
        valid = (lax.broadcasted_iota(jnp.int32, (BR, BR), 0) + t0 < len_ref[s]).astype(F32)
        x = x1_ref[pl.ds(r0, BR), :].astype(F32)
        h = x * (0.5 * (1.0 + lax.erf(x * 0.7071067811865476))) * valid
        hbuf[0, s, :, pl.ds(t0, BR)] = h.T.astype(BF16)

    for i in range(1, NX):
        wcopy(i).wait_recv()

    @pl.loop(1, 8)
    def _(i):
        wspread(i).start()

    loops.append((8, wspread))
    fetches[2].wait()

    @pl.loop(0, NS * LEN // BR)
    def _(i):
        s = i // (LEN // BR)
        t0 = pl.multiple_of((i % (LEN // BR)) * BR, BR)
        r0 = pl.multiple_of(i * BR, BR)
        valid = (lax.broadcasted_iota(jnp.int32, (BR, BR), 0) + t0 < len_ref[s]).astype(F32)
        x = x2_ref[pl.ds(r0, BR), :].astype(F32)
        phi = 0.5 * (1.0 + lax.erf(x * 0.7071067811865476))
        h2t[s, :, pl.ds(t0, BR)] = (x * phi * valid).T.astype(BF16)
        slope[pl.ds(r0, BR), :] = (phi + x * jnp.exp(-0.5 * x * x) * 0.3989422804014327) * valid

    xland(gpiece, gs_sem, gr_sem, 0)
    send(xcopy(gpiece, gs_sem, gr_sem, 5))
    xland(gpiece, gs_sem, gr_sem, 2)
    send(xcopy(gpiece, gs_sem, gr_sem, 4))

    def stack(src, slot, dilation):
        for s in range(NS):
            for k in range(KW):
                r0 = PAD - (k - KW // 2) * dilation
                gst[slot, s, :, k * BR : (k + 1) * BR] = src[s, r0 : r0 + LEN, :]

    def put_piece(kk, place, acts, slot):
        prod = jnp.dot(acts[0], gst[slot, 0], preferred_element_type=F32)
        prod += jnp.dot(acts[1], gst[slot, 1], preferred_element_type=F32)
        for k in range(KW):
            kbuf[kk, place, pl.ds(k, BR, stride=KW), :] = prod[:, k * BR : (k + 1) * BR]

    def second_piece(place):
        stack(gbuf.at[PLACES[place]], PLACES[place], 8)
        put_piece(1, place, h2t, PLACES[place])

    second_piece(0)
    xland(gpiece, gs_sem, gr_sem, 1)
    second_piece(1)
    xland(gpiece, gs_sem, gr_sem, 3)
    for i in (0, 2, 1, 3):
        send(xcopy(hpiece, hs_sem, hr_sem, i))
    second_piece(2)
    xland(gpiece, gs_sem, gr_sem, 4)
    xland(gpiece, gs_sem, gr_sem, 5)
    second_piece(3)

    sib = dp + 1 - 2 * c

    def ktile(u):
        kk, first, places = UNITS[u]
        return kbuf.at[kk].reshape(NX * KW, BR, BR).at[pl.ds(first * KW, places * KW)]

    def core_copy(u):
        other = pl.ds(pl.multiple_of((1 - c) * 64, 64), 64)
        return rcopy(
            ktile(u).at[:, other, :], core_in[u], c0_sem.at[2 * u], c0_sem.at[2 * u + 1], (sib, p)
        )

    def major_copy(u, t, land):
        return rcopy(
            ra[u].at[t] if land else pa[u].at[t], ra[u].at[t if land else a],
            s1_sem.at[u, t], r1_sem.at[u, t if land else a], (peer_at(t, b, c), p),
        )

    def minor_copy(u, t, land):
        return rcopy(
            rb[u].at[t] if land else pb[u], rb[u].at[t if land else b],
            s2_sem.at[u, t], r2_sem.at[u, t if land else b], (peer_at(a, t, c), p),
        )

    def to_major(u):
        core_copy(u).wait_recv()
        rows = UNITS[u][2] * KW * 8
        mine = pl.multiple_of(c * 64, 64)

        @pl.loop(0, 8)
        def _(t):
            t8 = pl.multiple_of(t * 8, 8)
            both = ktile(u)[:, pl.ds(mine + t8, 8), :] + core_in[u][:, pl.ds(t8, 8), :]
            both = both.reshape(rows, BR)
            if padded_rows(UNITS[u][2]) > rows:
                both = jnp.concatenate([both, jnp.zeros((8, BR), F32)], axis=0)
            pa[u][t] = both.astype(BF16)

        @pl.loop(1, 8)
        def _(i):
            major_copy(u, (a + i) % 8, False).start()

        loops.append((8, lambda i: major_copy(u, (a + i) % 8, False)))

    def to_minor(u):
        acc = pa[u][a].astype(F32)
        for i in range(1, 8):
            t = (a + i) % 8
            major_copy(u, t, True).wait_recv()
            acc = acc + ra[u][t].astype(F32)
        pb[u][...] = acc.astype(BF16)

        @pl.loop(1, 8)
        def _(i):
            minor_copy(u, (b + i) % 8, False).start()

        loops.append((8, lambda i: minor_copy(u, (b + i) % 8, False)))

    def minor_sum(u):
        acc = pb[u][...].astype(F32)
        for i in range(1, 8):
            t = (b + i) % 8
            minor_copy(u, t, True).wait_recv()
            acc = acc + rb[u][t].astype(F32)
        places = UNITS[u][2]
        return acc[: places * KW * 8].reshape(places, KW, 8, BR)

    send(core_copy(0))

    @pl.loop(1, 8)
    def _(i):
        wspread_land(i)

    fetches[3].wait()
    wcat = [jnp.concatenate([wbuf[slot, k] for k in range(KW)], axis=1) for slot in range(NX)]
    for s in range(NS):
        back = None
        for slot in range(NX):
            part = lax.dot_general(
                gst[slot, s], wcat[slot], (((1,), (1,)), ((), ())), preferred_element_type=F32
            )
            back = part if back is None else back + part
        g1[s, PAD : PAD + LEN, :] = (
            gbuf[0, s, PAD : PAD + LEN, :].astype(F32) + slope[s * LEN : (s + 1) * LEN, :] * back
        ).astype(BF16)
    to_major(0)
    stack(g1, NX, 4)

    def first_piece(place):
        put_piece(0, place, hbuf.at[PLACES[place]], NX)

    xland(hpiece, hs_sem, hr_sem, 0)
    send(xcopy(hpiece, hs_sem, hr_sem, 5))
    xland(hpiece, hs_sem, hr_sem, 2)
    send(xcopy(hpiece, hs_sem, hr_sem, 4))
    first_piece(0)

    def vcopy(i, land):
        q = (p + i) % NX
        at = i if land else NX - i
        return rcopy(rprev.at[at] if land else rprev.at[0], rprev.at[at], vs_sem.at[i], vr_sem.at[at], (dp, q))

    fetches[5].wait()
    for i in range(1, NX):
        send(vcopy(i, False))
    xland(hpiece, hs_sem, hr_sem, 1)
    first_piece(1)
    xland(hpiece, hs_sem, hr_sem, 3)
    first_piece(2)
    send(core_copy(1))
    to_major(1)
    xland(hpiece, hs_sem, hr_sem, 4)
    xland(hpiece, hs_sem, hr_sem, 5)
    first_piece(3)
    send(core_copy(2))
    to_major(2)
    to_minor(0)
    to_minor(1)
    to_minor(2)

    acc = minor_sum(0)
    for place in range(NX):
        p3[PLACES[place]] = acc[place]

    def piece_copy(i, land):
        q = (p + i) % NX
        return rcopy(
            r3.at[q] if land else p3.at[i], r3.at[q if land else p],
            s3_sem.at[i], r3_sem.at[q if land else p], (dp, q),
        )

    for i in range(1, NX):
        send(piece_copy(i, False))
    for u in (1, 2):
        acc = minor_sum(u)
        for k in range(UNITS[u][2]):
            q = (p + PLACES[UNITS[u][1] + k]) % NX
            rows_ref[pl.ds(q * KW, KW)] = acc[k]
    rows_ref[pl.ds((NX + p) * KW, KW)] = p3[0]
    for i in range(1, NX):
        piece_copy(i, True).wait_recv()
        q = (p + i) % NX
        rows_ref[pl.ds((NX + q) * KW, KW)] = r3[q]

    def line(i):
        return peer_at(i // 2, b, c) - c + i % 2

    for i in range(16):
        d4[i] = rows_ref[bos_ref[line(i)]]

    def group_copy(j):
        i = (a * 2 + c + j) % 16
        me = c * 8 + a
        return rcopy(d4.at[i], f4.at[me], fs_sem.at[i], fr_sem.at[me], (line(i), p))

    @pl.loop(1, 16)
    def _(j):
        group_copy(j).start()

    loops.append((16, group_copy))
    f4[c * 8 + a] = d4[a * 2 + c]

    @pl.loop(1, 16)
    def _(j):
        i = (c * 8 + a + j) % 16
        rcopy(f4.at[i], f4.at[i], fs_sem.at[i], fr_sem.at[i], (sib, p)).wait_recv()

    tiles[0] = f4[...].reshape(BR, BR).astype(BF16)

    def tile_copy(i, land):
        q = (p + i) % NX
        at = i if land else NX - i
        return rcopy(tiles.at[at] if land else tiles.at[0], tiles.at[at], ts_sem.at[i], tr_sem.at[at], (dp, q))

    for i in range(1, NX):
        send(tile_copy(i, False))
    for i in range(1, NX):
        vcopy(i, True).wait_recv()
    fetches[4].wait()
    for i in range(1, NX):
        tile_copy(i, True).wait_recv()

    tile = [tiles[i] for i in range(NX)]
    left_sum = None
    stats = []
    for i in range(NX):
        part = lax.dot_general(tile[i], tile[i], (((1,), (1,)), ((), ())), preferred_element_type=F32)
        left_sum = part if left_sum is None else left_sum + part
        gram = lax.dot_general(tile[i], tile[i], (((0,), (0,)), ((), ())), preferred_element_type=F32)
        stats.append(DECAY * rprev[i] + (1.0 - DECAY) * gram)
    stats.append(DECAY * lprev_ref[...] + (1.0 - DECAY) * left_sum)
    roots = [split(r) for r in inverse_fourth_roots(stats)]
    left_root = roots[NX]
    zero = jnp.zeros((BR, BR), BF16)
    raw = []
    for i in range(NX):
        mixed = split(mm(left_root, (tile[i], zero)) + mm((tile[i], zero), roots[i]))
        raw.append(mm(left_root, mixed) + mm(mixed, roots[i]))
    squares = raw[0] * raw[0]
    for i in range(1, NX):
        squares = squares + raw[i] * raw[i]
    total = jnp.sum(squares, axis=(0, 1), keepdims=True)
    inv = 1.0 / jnp.sqrt(total / (NX * BR * BR) + 1e-6)
    out_ref[...] = jnp.where(cnt_ref[0] > 0, raw[0] * inv, 0.0)

    drain()


def local(
    block_input, block_middle, out_grad, lengths, conv_weight, block_of_slot, slot_count, left_prev, right_prev
):
    vmem = pl.BlockSpec(memory_space=pltpu.VMEM)
    smem = pl.BlockSpec(memory_space=pltpu.SMEM)
    hbm = pl.BlockSpec(memory_space=pltpu.HBM)
    dma = pltpu.SemaphoreType.DMA
    out = pl.pallas_call(
        kernel,
        out_shape=jax.ShapeDtypeStruct((BR, BR), F32),
        in_specs=[hbm, hbm, hbm, smem, hbm, smem, smem, hbm, hbm],
        out_specs=vmem,
        scratch_shapes=[
            pltpu.VMEM((NS * LEN, BR), BF16),
            pltpu.VMEM((NS * LEN, BR), BF16),
            pltpu.VMEM((NS * LEN, BR), BF16),
            pltpu.VMEM((BR, BR), F32),
            pltpu.VMEM((NX, BR, BR), F32),
            pltpu.VMEM((NX, NS, LEN + 2 * PAD, BR), BF16),
            pltpu.VMEM((NX, NS, BR, LEN), BF16),
            pltpu.VMEM((NS, BR, LEN), BF16),
            pltpu.VMEM((NS * LEN, BR), F32),
            pltpu.VMEM((NX, KW, BR, BR), BF16),
            pltpu.VMEM((NX + 1, NS, LEN, KW * BR), BF16),
            pltpu.VMEM((NS, LEN + 2 * PAD, BR), BF16),
            pltpu.VMEM((2, NX, KW * BR, BR), F32),
            *[pltpu.VMEM((n * KW, 64, BR), F32) for _, _, n in UNITS],
            *[pltpu.VMEM((8, padded_rows(n), BR), BF16) for _, _, n in UNITS],
            *[pltpu.VMEM((8, padded_rows(n), BR), BF16) for _, _, n in UNITS],
            *[pltpu.VMEM((padded_rows(n), BR), BF16) for _, _, n in UNITS],
            *[pltpu.VMEM((8, padded_rows(n), BR), BF16) for _, _, n in UNITS],
            pltpu.VMEM((NX, KW, 8, BR), F32),
            pltpu.VMEM((NX, KW, 8, BR), F32),
            pltpu.VMEM((2 * NX * KW, 8, BR), F32),
            pltpu.VMEM((16, 8, BR), F32),
            pltpu.VMEM((16, 8, BR), F32),
            pltpu.VMEM((NX, BR, BR), BF16),
            dma((6,)), dma((6,)), dma((6,)), dma((6,)), dma((NX,)), dma((NX,)), dma((8,)), dma((8,)), dma((6,)),
            dma((3, 8)), dma((3, 8)), dma((3, 8)), dma((3, 8)), dma((NX,)), dma((NX,)),
            dma((16,)), dma((16,)), dma((NX,)), dma((NX,)), dma((NX,)), dma((NX,)), dma((6,)),
        ],
        compiler_params=pltpu.CompilerParams(
            collective_id=0, has_side_effects=True, vmem_limit_bytes=60 * 1024 * 1024
        ),
    )(
        block_input, block_middle, out_grad, lengths, conv_weight.transpose(1, 0, 2), block_of_slot,
        slot_count, left_prev.reshape(BR, BR), right_prev.reshape(BR, BR),
    )
    return out.reshape(1, BR * BR)


def solution(mesh):
    return jax.shard_map(
        local,
        mesh=mesh,
        in_specs=(
            P("dp", "owner"), P("dp", "owner"), P("dp", "owner"), P("dp"), P(None, None, "owner"), P(),
            P("dp"), P("dp", None), P("dp", "owner"),
        ),
        out_specs=P("dp", "owner"),
        check_vma=False,
    )
```

time: 96.9 us -> 72.3 us (0.75)
  Pallas kernels: 89 us -> 69.9 us
  local copies, waits for them, and re-layouts: 6.9 us -> 1.47 us
    pallas_call x1, Pallas kernels: 89 us -> 69.9 us  [local(): pl.pallas_call(kernel, out_shape=jax.ShapeDtypeStruct((BR, BR), F32), in_...]
    unnamed x17 -> x1, local copies, waits for them, and re-layouts: 6.9 us -> 1.47 us
where the time goes in v2:
time: 72.3 us; the launch traced here: 72.1 us
  Pallas kernels  69.9 us (97%)
  local copies, waits for them, and re-layouts  1.47 us (2%)
    pallas_call x1, Pallas kernels, local(): pl.pallas_call(kernel, out_shape=jax.ShapeDtypeStruct((BR, BR), F32), in_...  69.9 us
    unnamed x1, local copies, waits for them, and re-layouts  1.47 us

profile of v2, /device:TPU:1, one launch (start us, length us, event | category | flops | bytes accessed | tf_op | source)
XLA Modules:
  0.0 72.1 jit_solution(7814354920553234940)
XLA Ops:
  0.7 69.9 %shard_map.91 = f32[128,128]{1,0:T(8,128)} custom-call(bf16[1024,128]{1,0:T(8,128)(2,1)} %x1_hbm.1, bf16[1024,128]{1,0:T(8,128)(2,1)} %x2_hbm.1, bf16[1024,128]{1,0:T(8,128)(2,1)} %g_hbm.1, s32[2]{0:T(128)} %len_ref.1, bf16[5,512,128]{2,1,0:T(8,128)(2,1)} %bitcast.4, s32[128]{0:T(128)} %bos_ref.1, s32[1]{0:T(128)S(6)} %copy.11.cnt_ref, f32[128,128]{1,0:T(8,128)} %bitcast.6, ...), custom_call_target="tpu_custom_call" | custom-call | tf_op jit(solution)/shard_map/pallas_call | solution.py:472
  70.6 1.5 %copy.12 = f32[1,16384]{1,0:T(1,128)} copy(f32[1,16384]{1,0:T(1,128)} %bitcast.5) | data formatting | bytes 131072

commit v3 on v2

--- a/solution.py
+++ b/solution.py
@@ -58,7 +58,8 @@
 
 
 PLACES = (0, 3, 1, 2)
-UNITS = ((1, 0, 4), (0, 0, 3), (0, 3, 1))
+UNITS = ((1, 0, 3), (1, 3, 1), (0, 0, 3), (0, 3, 1))
+FAR = (4, 3, 5, 2, 6, 1, 7)
 
 
 def padded_rows(places):
@@ -66,10 +67,10 @@
 
 
 def kernel(
-    x1_hbm, x2_hbm, g_hbm, len_ref, w_ref, bos_ref, cnt_ref, lprev_hbm, rprev_hbm, out_ref,
-    x1_ref, x2_ref, g_ref, lprev_ref, rprev,
+    x1_hbm, x2_hbm, g_hbm, len_hbm, w_ref, bos_hbm, cnt_hbm, lprev_hbm, rprev_hbm, out_ref,
+    len_ref, bos_ref, cnt_ref, x1_ref, x2_ref, g_ref, lprev_ref, rprev,
     gbuf, hbuf, h2t, slope, wbuf, gst, g1, kbuf,
-    c0, c1, c2, pa0, pa1, pa2, ra0, ra1, ra2, pb0, pb1, pb2, rb0, rb1, rb2, p3, r3, rows_ref, d4, f4, tiles,
+    c0, c1, c2, c3, pa0, pa1, pa2, pa3, ra0, ra1, ra2, ra3, pb0, pb1, pb2, pb3, rb0, rb1, rb2, rb3, p3, r3, rows_ref, d4, f4, tiles,
     gs_sem, gr_sem, hs_sem, hr_sem, ws_sem, wr_sem, as_sem, ar_sem, c0_sem, s1_sem, r1_sem, s2_sem, r2_sem,
     s3_sem, r3_sem, fs_sem, fr_sem, vs_sem, vr_sem, ts_sem, tr_sem, in_sem,
 ):
@@ -80,8 +81,23 @@
     a = z + c * (y - z)
     b = y + c * (z - y)
     right, left = (p + 1) % NX, (p + 3) % NX
-    core_in, pa, ra = (c0, c1, c2), (pa0, pa1, pa2), (ra0, ra1, ra2)
-    pb, rb = (pb0, pb1, pb2), (rb0, rb1, rb2)
+    core_in, pa, ra = (c0, c1, c2, c3), (pa0, pa1, pa2, pa3), (ra0, ra1, ra2, ra3)
+    pb, rb = (pb0, pb1, pb2, pb3), (rb0, rb1, rb2, rb3)
+
+    barrier = pltpu.get_barrier_semaphore()
+
+    def greet(dev):
+        pl.semaphore_signal(barrier, inc=1, device_id=dev, device_id_type=MESH)
+
+    for step in FAR:
+        for core in range(2):
+            greet(((z * NY + (y + step) % NY) * 2 + core, p))
+    for step in (2, 1, 3):
+        greet((dp, (p + step) % NX))
+    for step in FAR:
+        for core in range(2):
+            greet(((((z + step) % NZ) * NY + y) * 2 + core, p))
+    greet((dp + 1 - 2 * c, p))
 
     def rcopy(src, dst, ss, rs, dev):
         return pltpu.make_async_remote_copy(
@@ -95,11 +111,12 @@
     fetches = [
         fetch(0, g_hbm, g_ref), fetch(1, x1_hbm, x1_ref), fetch(2, x2_hbm, x2_ref),
         fetch(3, w_ref.at[:, own, :], wbuf.at[0]), fetch(4, lprev_hbm, lprev_ref), fetch(5, rprev_hbm, rprev.at[0]),
+        fetch(6, len_hbm, len_ref), fetch(7, bos_hbm, bos_ref), fetch(8, cnt_hbm, cnt_ref),
     ]
-    for f in fetches:
-        f.start()
-
-    sent, loops = [], []
+    for i in (6, 0, 1, 2, 3, 4, 5, 7, 8):
+        fetches[i].start()
+
+    sent = []
 
     def send(copy):
         copy.start()
@@ -108,29 +125,6 @@
     def drain():
         for copy in sent:
             copy.wait_send()
-        for count, copy in loops:
-
-            @pl.loop(1, count)
-            def _(i):
-                copy(i).wait_send()
-
-    barrier = pltpu.get_barrier_semaphore()
-
-    def greet(dev):
-        pl.semaphore_signal(barrier, inc=1, device_id=dev, device_id_type=MESH)
-
-    @pl.loop(1, NX)
-    def _(i):
-        greet((dp, (p + i) % NX))
-
-    @pl.loop(1, 2 * NZ)
-    def _(i):
-        k = (z * 2 + c + i) % (2 * NZ)
-        greet((((k // 2) * NY + y) * 2 + k % 2, p))
-
-    @pl.loop(0, 2 * (NY - 1))
-    def _(i):
-        greet(((z * NY + (y + 1 + i // 2) % NY) * 2 + i % 2, p))
 
     zpad = jnp.zeros((PAD, BR), BF16)
     for slot in range(NX):
@@ -141,6 +135,7 @@
         g1[s, 0:PAD, :] = zpad
         g1[s, PAD + LEN : PAD + LEN + PAD, :] = zpad
     tok = lax.broadcasted_iota(jnp.int32, (LEN, BR), 0)
+    fetches[6].wait()
     fetches[0].wait()
     for s in range(NS):
         v = g_ref[s * LEN : (s + 1) * LEN, :].astype(F32)
@@ -184,10 +179,10 @@
         t = (a + i) % 8
         rcopy(wpart(t), wpart(t), as_sem.at[t], ar_sem.at[t], (peer_at(t, b, c), p)).wait_recv()
 
-    for i in range(1, NX):
-        send(wcopy(i))
     for i in (0, 2, 1, 3):
         send(xcopy(gpiece, gs_sem, gr_sem, i))
+    for i in (2, 1, 3):
+        send(wcopy(i))
 
     fetches[1].wait()
 
@@ -201,14 +196,6 @@
         h = x * (0.5 * (1.0 + lax.erf(x * 0.7071067811865476))) * valid
         hbuf[0, s, :, pl.ds(t0, BR)] = h.T.astype(BF16)
 
-    for i in range(1, NX):
-        wcopy(i).wait_recv()
-
-    @pl.loop(1, 8)
-    def _(i):
-        wspread(i).start()
-
-    loops.append((8, wspread))
     fetches[2].wait()
 
     @pl.loop(0, NS * LEN // BR)
@@ -222,11 +209,6 @@
         h2t[s, :, pl.ds(t0, BR)] = (x * phi * valid).T.astype(BF16)
         slope[pl.ds(r0, BR), :] = (phi + x * jnp.exp(-0.5 * x * x) * 0.3989422804014327) * valid
 
-    xland(gpiece, gs_sem, gr_sem, 0)
-    send(xcopy(gpiece, gs_sem, gr_sem, 5))
-    xland(gpiece, gs_sem, gr_sem, 2)
-    send(xcopy(gpiece, gs_sem, gr_sem, 4))
-
     def stack(src, slot, dilation):
         for s in range(NS):
             for k in range(KW):
@@ -242,17 +224,6 @@
     def second_piece(place):
         stack(gbuf.at[PLACES[place]], PLACES[place], 8)
         put_piece(1, place, h2t, PLACES[place])
-
-    second_piece(0)
-    xland(gpiece, gs_sem, gr_sem, 1)
-    second_piece(1)
-    xland(gpiece, gs_sem, gr_sem, 3)
-    for i in (0, 2, 1, 3):
-        send(xcopy(hpiece, hs_sem, hr_sem, i))
-    second_piece(2)
-    xland(gpiece, gs_sem, gr_sem, 4)
-    xland(gpiece, gs_sem, gr_sem, 5)
-    second_piece(3)
 
     sib = dp + 1 - 2 * c
 
@@ -292,11 +263,8 @@
                 both = jnp.concatenate([both, jnp.zeros((8, BR), F32)], axis=0)
             pa[u][t] = both.astype(BF16)
 
-        @pl.loop(1, 8)
-        def _(i):
-            major_copy(u, (a + i) % 8, False).start()
-
-        loops.append((8, lambda i: major_copy(u, (a + i) % 8, False)))
+        for step in FAR:
+            send(major_copy(u, (a + step) % 8, False))
 
     def to_minor(u):
         acc = pa[u][a].astype(F32)
@@ -306,11 +274,8 @@
             acc = acc + ra[u][t].astype(F32)
         pb[u][...] = acc.astype(BF16)
 
-        @pl.loop(1, 8)
-        def _(i):
-            minor_copy(u, (b + i) % 8, False).start()
-
-        loops.append((8, lambda i: minor_copy(u, (b + i) % 8, False)))
+        for step in FAR:
+            send(minor_copy(u, (b + step) % 8, False))
 
     def minor_sum(u):
         acc = pb[u][...].astype(F32)
@@ -321,62 +286,10 @@
         places = UNITS[u][2]
         return acc[: places * KW * 8].reshape(places, KW, 8, BR)
 
-    send(core_copy(0))
-
-    @pl.loop(1, 8)
-    def _(i):
-        wspread_land(i)
-
-    fetches[3].wait()
-    wcat = [jnp.concatenate([wbuf[slot, k] for k in range(KW)], axis=1) for slot in range(NX)]
-    for s in range(NS):
-        back = None
-        for slot in range(NX):
-            part = lax.dot_general(
-                gst[slot, s], wcat[slot], (((1,), (1,)), ((), ())), preferred_element_type=F32
-            )
-            back = part if back is None else back + part
-        g1[s, PAD : PAD + LEN, :] = (
-            gbuf[0, s, PAD : PAD + LEN, :].astype(F32) + slope[s * LEN : (s + 1) * LEN, :] * back
-        ).astype(BF16)
-    to_major(0)
-    stack(g1, NX, 4)
-
-    def first_piece(place):
-        put_piece(0, place, hbuf.at[PLACES[place]], NX)
-
-    xland(hpiece, hs_sem, hr_sem, 0)
-    send(xcopy(hpiece, hs_sem, hr_sem, 5))
-    xland(hpiece, hs_sem, hr_sem, 2)
-    send(xcopy(hpiece, hs_sem, hr_sem, 4))
-    first_piece(0)
-
     def vcopy(i, land):
         q = (p + i) % NX
         at = i if land else NX - i
         return rcopy(rprev.at[at] if land else rprev.at[0], rprev.at[at], vs_sem.at[i], vr_sem.at[at], (dp, q))
-
-    fetches[5].wait()
-    for i in range(1, NX):
-        send(vcopy(i, False))
-    xland(hpiece, hs_sem, hr_sem, 1)
-    first_piece(1)
-    xland(hpiece, hs_sem, hr_sem, 3)
-    first_piece(2)
-    send(core_copy(1))
-    to_major(1)
-    xland(hpiece, hs_sem, hr_sem, 4)
-    xland(hpiece, hs_sem, hr_sem, 5)
-    first_piece(3)
-    send(core_copy(2))
-    to_major(2)
-    to_minor(0)
-    to_minor(1)
-    to_minor(2)
-
-    acc = minor_sum(0)
-    for place in range(NX):
-        p3[PLACES[place]] = acc[place]
 
     def piece_copy(i, land):
         q = (p + i) % NX
@@ -385,35 +298,107 @@
             s3_sem.at[i], r3_sem.at[q if land else p], (dp, q),
         )
 
+
+    def first_piece(place):
+        put_piece(0, place, hbuf.at[PLACES[place]], NX)
+
+    def cotangent(s):
+        back = None
+        for slot in range(NX):
+            wcat = jnp.concatenate([wbuf[slot, k] for k in range(KW)], axis=1)
+            part = lax.dot_general(gst[slot, s], wcat, (((1,), (1,)), ((), ())), preferred_element_type=F32)
+            back = part if back is None else back + part
+        g1[s, PAD : PAD + LEN, :] = (
+            gbuf[0, s, PAD : PAD + LEN, :].astype(F32) + slope[s * LEN : (s + 1) * LEN, :] * back
+        ).astype(BF16)
+
+    second_piece(0)
     for i in range(1, NX):
-        send(piece_copy(i, False))
-    for u in (1, 2):
+        wcopy(i).wait_recv()
+    for step in FAR:
+        send(wspread(step))
+    xland(gpiece, gs_sem, gr_sem, 0)
+    send(xcopy(gpiece, gs_sem, gr_sem, 5))
+    xland(gpiece, gs_sem, gr_sem, 2)
+    send(xcopy(gpiece, gs_sem, gr_sem, 4))
+    xland(gpiece, gs_sem, gr_sem, 1)
+    xland(gpiece, gs_sem, gr_sem, 3)
+    for i in (0, 2, 1, 3):
+        send(xcopy(hpiece, hs_sem, hr_sem, i))
+    second_piece(1)
+    second_piece(2)
+    send(core_copy(0))
+    xland(gpiece, gs_sem, gr_sem, 4)
+    xland(gpiece, gs_sem, gr_sem, 5)
+    second_piece(3)
+    send(core_copy(1))
+    to_major(0)
+
+    @pl.loop(1, 8)
+    def _(i):
+        wspread_land(i)
+
+    fetches[3].wait()
+    cotangent(0)
+    to_major(1)
+    cotangent(1)
+    stack(g1, NX, 4)
+    first_piece(0)
+    xland(hpiece, hs_sem, hr_sem, 0)
+    send(xcopy(hpiece, hs_sem, hr_sem, 5))
+    xland(hpiece, hs_sem, hr_sem, 2)
+    send(xcopy(hpiece, hs_sem, hr_sem, 4))
+    xland(hpiece, hs_sem, hr_sem, 1)
+    first_piece(1)
+    xland(hpiece, hs_sem, hr_sem, 3)
+    first_piece(2)
+    send(core_copy(2))
+    to_minor(0)
+    to_major(2)
+    xland(hpiece, hs_sem, hr_sem, 4)
+    xland(hpiece, hs_sem, hr_sem, 5)
+    first_piece(3)
+    send(core_copy(3))
+    fetches[5].wait()
+    for i in (2, 1, 3):
+        send(vcopy(i, False))
+    to_minor(1)
+    to_major(3)
+    to_minor(2)
+
+    for u in (0, 1):
         acc = minor_sum(u)
         for k in range(UNITS[u][2]):
-            q = (p + PLACES[UNITS[u][1] + k]) % NX
-            rows_ref[pl.ds(q * KW, KW)] = acc[k]
+            p3[PLACES[UNITS[u][1] + k]] = acc[k]
+    for i in (2, 1, 3):
+        send(piece_copy(i, False))
+    to_minor(3)
     rows_ref[pl.ds((NX + p) * KW, KW)] = p3[0]
     for i in range(1, NX):
         piece_copy(i, True).wait_recv()
         q = (p + i) % NX
         rows_ref[pl.ds((NX + q) * KW, KW)] = r3[q]
+    for u in (2, 3):
+        acc = minor_sum(u)
+        for k in range(UNITS[u][2]):
+            q = (p + PLACES[UNITS[u][1] + k]) % NX
+            rows_ref[pl.ds(q * KW, KW)] = acc[k]
 
     def line(i):
         return peer_at(i // 2, b, c) - c + i % 2
 
+    fetches[7].wait()
     for i in range(16):
         d4[i] = rows_ref[bos_ref[line(i)]]
 
-    def group_copy(j):
-        i = (a * 2 + c + j) % 16
+    def group_copy(i):
         me = c * 8 + a
         return rcopy(d4.at[i], f4.at[me], fs_sem.at[i], fr_sem.at[me], (line(i), p))
 
-    @pl.loop(1, 16)
-    def _(j):
-        group_copy(j).start()
-
-    loops.append((16, group_copy))
+    for step in FAR:
+        for core in range(2):
+            send(group_copy((a + step) % 8 * 2 + core))
+    send(group_copy(a * 2 + 1 - c))
     f4[c * 8 + a] = d4[a * 2 + c]
 
     @pl.loop(1, 16)
@@ -428,11 +413,12 @@
         at = i if land else NX - i
         return rcopy(tiles.at[at] if land else tiles.at[0], tiles.at[at], ts_sem.at[i], tr_sem.at[at], (dp, q))
 
-    for i in range(1, NX):
+    for i in (2, 1, 3):
         send(tile_copy(i, False))
     for i in range(1, NX):
         vcopy(i, True).wait_recv()
     fetches[4].wait()
+    fetches[8].wait()
     for i in range(1, NX):
         tile_copy(i, True).wait_recv()
 
@@ -466,15 +452,17 @@
     block_input, block_middle, out_grad, lengths, conv_weight, block_of_slot, slot_count, left_prev, right_prev
 ):
     vmem = pl.BlockSpec(memory_space=pltpu.VMEM)
-    smem = pl.BlockSpec(memory_space=pltpu.SMEM)
     hbm = pl.BlockSpec(memory_space=pltpu.HBM)
     dma = pltpu.SemaphoreType.DMA
     out = pl.pallas_call(
         kernel,
         out_shape=jax.ShapeDtypeStruct((BR, BR), F32),
-        in_specs=[hbm, hbm, hbm, smem, hbm, smem, smem, hbm, hbm],
+        in_specs=[hbm] * 9,
         out_specs=vmem,
         scratch_shapes=[
+            pltpu.SMEM((NS,), jnp.int32),
+            pltpu.SMEM((BR,), jnp.int32),
+            pltpu.SMEM((1,), jnp.int32),
             pltpu.VMEM((NS * LEN, BR), BF16),
             pltpu.VMEM((NS * LEN, BR), BF16),
             pltpu.VMEM((NS * LEN, BR), BF16),
@@ -499,9 +487,9 @@
             pltpu.VMEM((16, 8, BR), F32),
             pltpu.VMEM((16, 8, BR), F32),
             pltpu.VMEM((NX, BR, BR), BF16),
-            dma((6,)), dma((6,)), dma((6,)), dma((6,)), dma((NX,)), dma((NX,)), dma((8,)), dma((8,)), dma((6,)),
-            dma((3, 8)), dma((3, 8)), dma((3, 8)), dma((3, 8)), dma((NX,)), dma((NX,)),
-            dma((16,)), dma((16,)), dma((NX,)), dma((NX,)), dma((NX,)), dma((NX,)), dma((6,)),
+            dma((6,)), dma((6,)), dma((6,)), dma((6,)), dma((NX,)), dma((NX,)), dma((8,)), dma((8,)), dma((8,)),
+            dma((4, 8)), dma((4, 8)), dma((4, 8)), dma((4, 8)), dma((NX,)), dma((NX,)),
+            dma((16,)), dma((16,)), dma((NX,)), dma((NX,)), dma((NX,)), dma((NX,)), dma((9,)),
         ],
         compiler_params=pltpu.CompilerParams(
             collective_id=0, has_side_effects=True, vmem_limit_bytes=60 * 1024 * 1024

time: 72.3 us -> 71.3 us (0.986)
  Pallas kernels: 69.9 us -> 69 us
    pallas_call x1, Pallas kernels: 69.9 us -> 69 us  [local(): pl.pallas_call(kernel, out_shape=jax.ShapeDtypeStruct((BR, BR), F32), in_...]
where the time goes in v3:
time: 71.3 us; the launch traced here: 71.1 us
  Pallas kernels  69 us (97%)
  local copies, waits for them, and re-layouts  1.47 us (2%)
    pallas_call x1, Pallas kernels, local(): pl.pallas_call(kernel, out_shape=jax.ShapeDtypeStruct((BR, BR), F32), in_...  69 us
    unnamed x1, local copies, waits for them, and re-layouts  1.47 us

profile of v3, /device:TPU:1, one launch (start us, length us, event | category | flops | bytes accessed | tf_op | source)
XLA Modules:
  0.0 71.1 jit_solution(7545131155888093861)
XLA Ops:
  0.7 69.0 %shard_map.91 = f32[128,128]{1,0:T(8,128)} custom-call(bf16[1024,128]{1,0:T(8,128)(2,1)} %x1_hbm.1, bf16[1024,128]{1,0:T(8,128)(2,1)} %x2_hbm.1, bf16[1024,128]{1,0:T(8,128)(2,1)} %g_hbm.1, s32[2]{0:T(128)} %len_hbm.1, bf16[5,512,128]{2,1,0:T(8,128)(2,1)} %bitcast.4, s32[128]{0:T(128)} %bos_hbm.1, s32[1]{0:T(128)S(6)} %copy.11.cnt_hbm, f32[128,128]{1,0:T(8,128)} %bitcast.6, ...), custom_call_target="tpu_custom_call" | custom-call | tf_op jit(solution)/shard_map/pallas_call | solution.py:457
  69.7 1.5 %copy.12 = f32[1,16384]{1,0:T(1,128)} copy(f32[1,16384]{1,0:T(1,128)} %bitcast.5) | data formatting | bytes 131072

commit v4 on v3

--- a/solution.py
+++ b/solution.py
@@ -30,6 +30,10 @@
     )
     both = jnp.dot(left, right, preferred_element_type=F32)
     return both[:, :BR] + both[:, BR:]
+
+
+def bdot(a, b):
+    return jnp.dot(a, b, preferred_element_type=F32)
 
 
 def inverse_fourth_roots(stats):
@@ -44,8 +48,8 @@
         parts = [split(f) for f in fac]
         if it < ITERS - 1:
             square = [split(mm(f, f)) for f in parts]
-            fourth = [split(mm(s, s)) for s in square]
-            cur = [mm(f, split(m)) for f, m in zip(fourth, cur)]
+            half = [split(mm(s, split(m))) for s, m in zip(square, cur)]
+            cur = [mm(h, s) for h, s in zip(half, square)]
         root = fac if it == 0 else [mm(split(r), f) for r, f in zip(root, parts)]
     scale = [1.0 / jnp.sqrt(jnp.sqrt(n)) for n in norms]
     return [r * s for r, s in zip(root, scale)]
@@ -179,10 +183,10 @@
         t = (a + i) % 8
         rcopy(wpart(t), wpart(t), as_sem.at[t], ar_sem.at[t], (peer_at(t, b, c), p)).wait_recv()
 
+    for i in (2, 1, 3):
+        send(wcopy(i))
     for i in (0, 2, 1, 3):
         send(xcopy(gpiece, gs_sem, gr_sem, i))
-    for i in (2, 1, 3):
-        send(wcopy(i))
 
     fetches[1].wait()
 
@@ -254,8 +258,7 @@
         rows = UNITS[u][2] * KW * 8
         mine = pl.multiple_of(c * 64, 64)
 
-        @pl.loop(0, 8)
-        def _(t):
+        def fill(t):
             t8 = pl.multiple_of(t * 8, 8)
             both = ktile(u)[:, pl.ds(mine + t8, 8), :] + core_in[u][:, pl.ds(t8, 8), :]
             both = both.reshape(rows, BR)
@@ -264,7 +267,10 @@
             pa[u][t] = both.astype(BF16)
 
         for step in FAR:
-            send(major_copy(u, (a + step) % 8, False))
+            t = (a + step) % 8
+            fill(t)
+            send(major_copy(u, t, False))
+        fill(a)
 
     def to_minor(u):
         acc = pa[u][a].astype(F32)
@@ -362,8 +368,8 @@
     fetches[5].wait()
     for i in (2, 1, 3):
         send(vcopy(i, False))
+    to_major(3)
     to_minor(1)
-    to_major(3)
     to_minor(2)
 
     for u in (0, 1):
@@ -413,6 +419,8 @@
         at = i if land else NX - i
         return rcopy(tiles.at[at] if land else tiles.at[0], tiles.at[at], ts_sem.at[i], tr_sem.at[at], (dp, q))
 
+    drain()
+    sent.clear()
     for i in (2, 1, 3):
         send(tile_copy(i, False))
     for i in range(1, NX):
@@ -434,16 +442,16 @@
     roots = [split(r) for r in inverse_fourth_roots(stats)]
     left_root = roots[NX]
     zero = jnp.zeros((BR, BR), BF16)
-    raw = []
-    for i in range(NX):
-        mixed = split(mm(left_root, (tile[i], zero)) + mm((tile[i], zero), roots[i]))
-        raw.append(mm(left_root, mixed) + mm(mixed, roots[i]))
-    squares = raw[0] * raw[0]
+    mixed = split(mm(left_root, (tile[0], zero)) + mm((tile[0], zero), roots[0]))
+    raw = mm(left_root, mixed) + mm(mixed, roots[0])
+    squares = raw * raw
     for i in range(1, NX):
-        squares = squares + raw[i] * raw[i]
+        mixed = (bdot(left_root[0], tile[i]) + bdot(tile[i], roots[i][0])).astype(BF16)
+        other = bdot(left_root[0], mixed) + bdot(mixed, roots[i][0])
+        squares = squares + other * other
     total = jnp.sum(squares, axis=(0, 1), keepdims=True)
     inv = 1.0 / jnp.sqrt(total / (NX * BR * BR) + 1e-6)
-    out_ref[...] = jnp.where(cnt_ref[0] > 0, raw[0] * inv, 0.0)
+    out_ref[...] = jnp.where(cnt_ref[0] > 0, raw * inv, 0.0)
 
     drain()
 

time: 71.3 us -> 67.6 us (0.948)
  Pallas kernels: 69 us -> 65.3 us
    pallas_call x1, Pallas kernels: 69 us -> 65.3 us  [local(): pl.pallas_call(kernel, out_shape=jax.ShapeDtypeStruct((BR, BR), F32), in_...]
where the time goes in v4:
time: 67.6 us; the launch traced here: 67.4 us
  Pallas kernels  65.3 us (97%)
  local copies, waits for them, and re-layouts  1.47 us (2%)
    pallas_call x1, Pallas kernels, local(): pl.pallas_call(kernel, out_shape=jax.ShapeDtypeStruct((BR, BR), F32), in_...  65.3 us
    unnamed x1, local copies, waits for them, and re-layouts  1.47 us

profile of v4, /device:TPU:1, one launch (start us, length us, event | category | flops | bytes accessed | tf_op | source)
XLA Modules:
  0.0 67.4 jit_solution(6958654090926563035)
XLA Ops:
  0.7 65.3 %shard_map.91 = f32[128,128]{1,0:T(8,128)} custom-call(bf16[1024,128]{1,0:T(8,128)(2,1)} %x1_hbm.1, bf16[1024,128]{1,0:T(8,128)(2,1)} %x2_hbm.1, bf16[1024,128]{1,0:T(8,128)(2,1)} %g_hbm.1, s32[2]{0:T(128)} %len_hbm.1, bf16[5,512,128]{2,1,0:T(8,128)(2,1)} %bitcast.4, s32[128]{0:T(128)} %bos_hbm.1, s32[1]{0:T(128)S(6)} %copy.11.cnt_hbm, f32[128,128]{1,0:T(8,128)} %bitcast.6, ...), custom_call_target="tpu_custom_call" | custom-call | tf_op jit(solution)/shard_map/pallas_call | solution.py:465
  65.9 1.5 %copy.12 = f32[1,16384]{1,0:T(1,128)} copy(f32[1,16384]{1,0:T(1,128)} %bitcast.5) | data formatting | bytes 131072

commit v5 on v4

--- a/solution.py
+++ b/solution.py
@@ -76,7 +76,7 @@
     gbuf, hbuf, h2t, slope, wbuf, gst, g1, kbuf,
     c0, c1, c2, c3, pa0, pa1, pa2, pa3, ra0, ra1, ra2, ra3, pb0, pb1, pb2, pb3, rb0, rb1, rb2, rb3, p3, r3, rows_ref, d4, f4, tiles,
     gs_sem, gr_sem, hs_sem, hr_sem, ws_sem, wr_sem, as_sem, ar_sem, c0_sem, s1_sem, r1_sem, s2_sem, r2_sem,
-    s3_sem, r3_sem, fs_sem, fr_sem, vs_sem, vr_sem, ts_sem, tr_sem, in_sem,
+    s3_sem, r3_sem, fs_sem, fr_sem, vs_sem, vr_sem, ts_sem, tr_sem, in_sem, word_sem,
 ):
     dp, p = lax.axis_index("dp"), lax.axis_index("owner")
     c = dp % 2
@@ -93,15 +93,20 @@
     def greet(dev):
         pl.semaphore_signal(barrier, inc=1, device_id=dev, device_id_type=MESH)
 
-    for step in FAR:
-        for core in range(2):
-            greet(((z * NY + (y + step) % NY) * 2 + core, p))
+    near = [((z * NY + (y + step) % NY) * 2 + c, p) for step in (1, 7)]
+    near += [((((z + step) % NZ) * NY + y) * 2 + c, p) for step in (1, 7)]
+    for dev in near:
+        greet(dev)
     for step in (2, 1, 3):
         greet((dp, (p + step) % NX))
-    for step in FAR:
-        for core in range(2):
-            greet(((((z + step) % NZ) * NY + y) * 2 + core, p))
     greet((dp + 1 - 2 * c, p))
+
+    def tell(k):
+        for dev in near:
+            pl.semaphore_signal(word_sem.at[k], inc=1, device_id=dev, device_id_type=MESH)
+
+    def heard(k):
+        pl.semaphore_wait(word_sem.at[k], 4)
 
     def rcopy(src, dst, ss, rs, dev):
         return pltpu.make_async_remote_copy(
@@ -145,7 +150,7 @@
         v = g_ref[s * LEN : (s + 1) * LEN, :].astype(F32)
         gbuf[0, s, PAD : PAD + LEN, :] = jnp.where(tok < len_ref[s], v, 0.0).astype(BF16)
 
-    pl.semaphore_wait(barrier, 3 + 15 + 14)
+    pl.semaphore_wait(barrier, 4 + 3 + 1)
 
     def gpiece(slot, s):
         return gbuf.at[slot, s, pl.ds(PAD, LEN), :]
@@ -187,6 +192,8 @@
         send(wcopy(i))
     for i in (0, 2, 1, 3):
         send(xcopy(gpiece, gs_sem, gr_sem, i))
+
+    tell(0)
 
     fetches[1].wait()
 
@@ -200,6 +207,8 @@
         h = x * (0.5 * (1.0 + lax.erf(x * 0.7071067811865476))) * valid
         hbuf[0, s, :, pl.ds(t0, BR)] = h.T.astype(BF16)
 
+    heard(0)
+    tell(1)
     fetches[2].wait()
 
     @pl.loop(0, NS * LEN // BR)
@@ -318,9 +327,12 @@
             gbuf[0, s, PAD : PAD + LEN, :].astype(F32) + slope[s * LEN : (s + 1) * LEN, :] * back
         ).astype(BF16)
 
+    heard(1)
+    tell(2)
     second_piece(0)
     for i in range(1, NX):
         wcopy(i).wait_recv()
+    heard(2)
     for step in FAR:
         send(wspread(step))
     xland(gpiece, gs_sem, gr_sem, 0)
@@ -339,7 +351,6 @@
     second_piece(3)
     send(core_copy(1))
     to_major(0)
-
     @pl.loop(1, 8)
     def _(i):
         wspread_land(i)
@@ -371,14 +382,13 @@
     to_major(3)
     to_minor(1)
     to_minor(2)
-
+    to_minor(3)
     for u in (0, 1):
         acc = minor_sum(u)
         for k in range(UNITS[u][2]):
             p3[PLACES[UNITS[u][1] + k]] = acc[k]
     for i in (2, 1, 3):
         send(piece_copy(i, False))
-    to_minor(3)
     rows_ref[pl.ds((NX + p) * KW, KW)] = p3[0]
     for i in range(1, NX):
         piece_copy(i, True).wait_recv()
@@ -498,6 +508,7 @@
             dma((6,)), dma((6,)), dma((6,)), dma((6,)), dma((NX,)), dma((NX,)), dma((8,)), dma((8,)), dma((8,)),
             dma((4, 8)), dma((4, 8)), dma((4, 8)), dma((4, 8)), dma((NX,)), dma((NX,)),
             dma((16,)), dma((16,)), dma((NX,)), dma((NX,)), dma((NX,)), dma((NX,)), dma((9,)),
+            pltpu.SemaphoreType.REGULAR((3,)),
         ],
         compiler_params=pltpu.CompilerParams(
             collective_id=0, has_side_effects=True, vmem_limit_bytes=60 * 1024 * 1024

time: 67.6 us -> 66.4 us (0.982)
  Pallas kernels: 65.3 us -> 64.1 us
    pallas_call x1, Pallas kernels: 65.3 us -> 64.1 us  [local(): pl.pallas_call(kernel, out_shape=jax.ShapeDtypeStruct((BR, BR), F32), in_...]
where the time goes in v5:
time: 66.4 us; the launch traced here: 66.3 us
  Pallas kernels  64.1 us (97%)
  local copies, waits for them, and re-layouts  1.47 us (2%)
    pallas_call x1, Pallas kernels, local(): pl.pallas_call(kernel, out_shape=jax.ShapeDtypeStruct((BR, BR), F32), in_...  64.1 us
    unnamed x1, local copies, waits for them, and re-layouts  1.47 us

profile of v5, /device:TPU:1, one launch (start us, length us, event | category | flops | bytes accessed | tf_op | source)
XLA Modules:
  0.0 66.3 jit_solution(15948494800485443151)
XLA Ops:
  0.7 64.1 %shard_map.91 = f32[128,128]{1,0:T(8,128)} custom-call(bf16[1024,128]{1,0:T(8,128)(2,1)} %x1_hbm.1, bf16[1024,128]{1,0:T(8,128)(2,1)} %x2_hbm.1, bf16[1024,128]{1,0:T(8,128)(2,1)} %g_hbm.1, s32[2]{0:T(128)} %len_hbm.1, bf16[5,512,128]{2,1,0:T(8,128)(2,1)} %bitcast.4, s32[128]{0:T(128)} %bos_hbm.1, s32[1]{0:T(128)S(6)} %copy.11.cnt_hbm, f32[128,128]{1,0:T(8,128)} %bitcast.6, ...), custom_call_target="tpu_custom_call" | custom-call | tf_op jit(solution)/shard_map/pallas_call | solution.py:475
  64.8 1.5 %copy.12 = f32[1,16384]{1,0:T(1,128)} copy(f32[1,16384]{1,0:T(1,128)} %bitcast.5) | data formatting | bytes 131072

commit v6 on v5

--- a/solution.py
+++ b/solution.py
@@ -80,11 +80,11 @@
 ):
     dp, p = lax.axis_index("dp"), lax.axis_index("owner")
     c = dp % 2
+    right, left = (p + 1) % NX, (p + 3) % NX
     y = (dp // 2) % NY
     z = dp // (2 * NY)
     a = z + c * (y - z)
     b = y + c * (z - y)
-    right, left = (p + 1) % NX, (p + 3) % NX
     core_in, pa, ra = (c0, c1, c2, c3), (pa0, pa1, pa2, pa3), (ra0, ra1, ra2, ra3)
     pb, rb = (pb0, pb1, pb2, pb3), (rb0, rb1, rb2, rb3)
 
@@ -95,10 +95,9 @@
 
     near = [((z * NY + (y + step) % NY) * 2 + c, p) for step in (1, 7)]
     near += [((((z + step) % NZ) * NY + y) * 2 + c, p) for step in (1, 7)]
+    near += [(dp, right), (dp, left)]
     for dev in near:
         greet(dev)
-    for step in (2, 1, 3):
-        greet((dp, (p + step) % NX))
     greet((dp + 1 - 2 * c, p))
 
     def tell(k):
@@ -106,7 +105,7 @@
             pl.semaphore_signal(word_sem.at[k], inc=1, device_id=dev, device_id_type=MESH)
 
     def heard(k):
-        pl.semaphore_wait(word_sem.at[k], 4)
+        pl.semaphore_wait(word_sem.at[k], 6)
 
     def rcopy(src, dst, ss, rs, dev):
         return pltpu.make_async_remote_copy(
@@ -150,7 +149,7 @@
         v = g_ref[s * LEN : (s + 1) * LEN, :].astype(F32)
         gbuf[0, s, PAD : PAD + LEN, :] = jnp.where(tok < len_ref[s], v, 0.0).astype(BF16)
 
-    pl.semaphore_wait(barrier, 4 + 3 + 1)
+    pl.semaphore_wait(barrier, 4 + 2 + 1)
 
     def gpiece(slot, s):
         return gbuf.at[slot, s, pl.ds(PAD, LEN), :]
@@ -188,9 +187,9 @@
         t = (a + i) % 8
         rcopy(wpart(t), wpart(t), as_sem.at[t], ar_sem.at[t], (peer_at(t, b, c), p)).wait_recv()
 
-    for i in (2, 1, 3):
+    for i in (1, 3):
         send(wcopy(i))
-    for i in (0, 2, 1, 3):
+    for i in (0, 2):
         send(xcopy(gpiece, gs_sem, gr_sem, i))
 
     tell(0)
@@ -208,6 +207,9 @@
         hbuf[0, s, :, pl.ds(t0, BR)] = h.T.astype(BF16)
 
     heard(0)
+    send(wcopy(2))
+    for i in (1, 3):
+        send(xcopy(gpiece, gs_sem, gr_sem, i))
     tell(1)
     fetches[2].wait()
 
@@ -429,10 +431,11 @@
         at = i if land else NX - i
         return rcopy(tiles.at[at] if land else tiles.at[0], tiles.at[at], ts_sem.at[i], tr_sem.at[at], (dp, q))
 
+    for i in (2, 1, 3):
+        tile_copy(i, False).start()
     drain()
     sent.clear()
-    for i in (2, 1, 3):
-        send(tile_copy(i, False))
+    sent.extend(tile_copy(i, False) for i in (2, 1, 3))
     for i in range(1, NX):
         vcopy(i, True).wait_recv()
     fetches[4].wait()

time: 66.4 us -> 65.6 us (0.988)
  Pallas kernels: 64.1 us -> 63.2 us
    pallas_call x1, Pallas kernels: 64.1 us -> 63.2 us  [local(): pl.pallas_call(kernel, out_shape=jax.ShapeDtypeStruct((BR, BR), F32), in_...]
where the time goes in v6:
time: 65.6 us; the launch traced here: 65.4 us
  Pallas kernels  63.2 us (96%)
  local copies, waits for them, and re-layouts  1.47 us (2%)
  between operations  0.66 us (1%)
    pallas_call x1, Pallas kernels, local(): pl.pallas_call(kernel, out_shape=jax.ShapeDtypeStruct((BR, BR), F32), in_...  63.2 us
    unnamed x1, local copies, waits for them, and re-layouts  1.47 us

profile of v6, /device:TPU:1, one launch (start us, length us, event | category | flops | bytes accessed | tf_op | source)
XLA Modules:
  0.0 65.4 jit_solution(15643793105340535591)
XLA Ops:
  0.7 63.2 %shard_map.91 = f32[128,128]{1,0:T(8,128)} custom-call(bf16[1024,128]{1,0:T(8,128)(2,1)} %x1_hbm.1, bf16[1024,128]{1,0:T(8,128)(2,1)} %x2_hbm.1, bf16[1024,128]{1,0:T(8,128)(2,1)} %g_hbm.1, s32[2]{0:T(128)} %len_hbm.1, bf16[5,512,128]{2,1,0:T(8,128)(2,1)} %bitcast.4, s32[128]{0:T(128)} %bos_hbm.1, s32[1]{0:T(128)S(6)} %copy.11.cnt_hbm, f32[128,128]{1,0:T(8,128)} %bitcast.6, ...), custom_call_target="tpu_custom_call" | custom-call | tf_op jit(solution)/shard_map/pallas_call | solution.py:478
  63.9 1.5 %copy.12 = f32[1,16384]{1,0:T(1,128)} copy(f32[1,16384]{1,0:T(1,128)} %bitcast.5) | data formatting | bytes 131072

commit v7 on v6

--- a/solution.py
+++ b/solution.py
@@ -341,9 +341,11 @@
     send(xcopy(gpiece, gs_sem, gr_sem, 5))
     xland(gpiece, gs_sem, gr_sem, 2)
     send(xcopy(gpiece, gs_sem, gr_sem, 4))
+    for i in (0, 2):
+        send(xcopy(hpiece, hs_sem, hr_sem, i))
     xland(gpiece, gs_sem, gr_sem, 1)
     xland(gpiece, gs_sem, gr_sem, 3)
-    for i in (0, 2, 1, 3):
+    for i in (1, 3):
         send(xcopy(hpiece, hs_sem, hr_sem, i))
     second_piece(1)
     second_piece(2)

time: 65.6 us -> 65.2 us (level)
  no operation moved by 1% of the time
where the time goes in v7:
time: 65.2 us; the launch traced here: 65 us
  Pallas kernels  62.9 us (96%)
  local copies, waits for them, and re-layouts  1.47 us (2%)
  between operations  0.66 us (1%)
    pallas_call x1, Pallas kernels, local(): pl.pallas_call(kernel, out_shape=jax.ShapeDtypeStruct((BR, BR), F32), in_...  62.9 us
    unnamed x1, local copies, waits for them, and re-layouts  1.47 us

profile of v7, /device:TPU:1, one launch (start us, length us, event | category | flops | bytes accessed | tf_op | source)
XLA Modules:
  0.0 65.0 jit_solution(10197461568003539251)
XLA Ops:
  0.7 62.9 %shard_map.91 = f32[128,128]{1,0:T(8,128)} custom-call(bf16[1024,128]{1,0:T(8,128)(2,1)} %x1_hbm.1, bf16[1024,128]{1,0:T(8,128)(2,1)} %x2_hbm.1, bf16[1024,128]{1,0:T(8,128)(2,1)} %g_hbm.1, s32[2]{0:T(128)} %len_hbm.1, bf16[5,512,128]{2,1,0:T(8,128)(2,1)} %bitcast.4, s32[128]{0:T(128)} %bos_hbm.1, s32[1]{0:T(128)S(6)} %copy.11.cnt_hbm, f32[128,128]{1,0:T(8,128)} %bitcast.6, ...), custom_call_target="tpu_custom_call" | custom-call | tf_op jit(solution)/shard_map/pallas_call | solution.py:480
  63.5 1.5 %copy.12 = f32[1,16384]{1,0:T(1,128)} copy(f32[1,16384]{1,0:T(1,128)} %bitcast.5) | data formatting | bytes 131072
